TPU v7x, 32 devices: a whole 2x2x4 slice. The times are simulated.
32 devices in a mesh: dp: 16 (over z, y, x), tensor: 2 (over core).
Axes of the slice: x: 2, y: 2, z: 4, core: 2. Of those that a mesh axis runs over, the one named last changes fastest.
Arguments:
- tokens: bfloat16 [512, 144, 384], P('dp', 'tensor'), may hold values from -6 to 6
- token_mask: int32 [512, 144], P('dp'), may hold values from 0 to 1, as said below
- shift_next: int32 [512], P('dp'), may hold values from 0 to 31, as said below
- cotangent: bfloat16 [512, 144, 384], P('dp', 'tensor'), may hold values from -6 to 6
- attend_gain: float32 [2, 384], replicated, may hold values from 0.1 to 1.9
- attend_shift: float32 [2, 384], replicated, may hold values from -1.5 to 1.5
- inward_weight: bfloat16 [2, 384, 3, 384], P(None, None, None, 'tensor'), may hold values from -0.3125 to 0.3125
- inward_bias: float32 [2, 2, 384], P(None, None, 'tensor'), may hold values from -1.5 to 1.5
- earth_bias: float32 [2, 12, 144, 144], P(None, 'tensor'), may hold values from -5 to 5
- outward_weight: bfloat16 [2, 384, 384], P(None, 'tensor'), may hold values from -0.875 to 0.875
- outward_bias: float32 [2, 384], replicated, may hold values from -1.5 to 1.5
- mixer_gain: float32 [2, 384], replicated, may hold values from 0.1 to 1.9
- mixer_shift: float32 [2, 384], replicated, may hold values from -1.5 to 1.5
- up_weight: bfloat16 [2, 384, 1536], P(None, None, 'tensor'), may hold values from -0.3125 to 0.3125
- up_bias: float32 [2, 1536], P(None, 'tensor'), may hold values from -1.5 to 1.5
- down_weight: bfloat16 [2, 1536, 384], P(None, 'tensor'), may hold values from -0.21875 to 0.21875
- down_bias: float32 [2, 384], replicated, may hold values from -1.5 to 1.5
Outputs:
- block_output: bfloat16 [512, 144, 384], P('dp', 'tensor')
- tokens_grad: bfloat16 [512, 144, 384], P('dp', 'tensor')
- attend_gain_grad: float32 [2, 384], replicated
- attend_shift_grad: float32 [2, 384], replicated
- inward_weight_grad: float32 [2, 384, 3, 384], P(None, None, None, 'tensor')
- inward_bias_grad: float32 [2, 2, 384], P(None, None, 'tensor')
- earth_bias_grad: float32 [2, 12, 144, 144], P(None, 'tensor')
- outward_weight_grad: float32 [2, 384, 384], P(None, 'tensor')
- outward_bias_grad: float32 [2, 384], replicated
- mixer_gain_grad: float32 [2, 384], replicated
- mixer_shift_grad: float32 [2, 384], replicated
- up_weight_grad: float32 [2, 384, 1536], P(None, None, 'tensor')
- up_bias_grad: float32 [2, 1536], P(None, 'tensor')
- down_weight_grad: float32 [2, 1536, 384], P(None, 'tensor')
- down_bias_grad: float32 [2, 384], replicated
Inputs may be any that keep to these rules, and one draw needn't show every extreme that they name: `token_mask`: A window slot is live if it holds a valid token, dead if it holds none. Each device's 32 slots hold from 0 to 32 live windows, and some device holds 32; the live windows of all devices number exactly 16 times the devices of dp. The valid tokens of a live window are those of latitude row below some r (1 to 6) and longitude column below some c (1 to 12). `shift_next`: each device's 32 entries are a permutation of its slots 0 to 31: a live window goes to the next live window of its crop row on the same device, the last to the first, and a dead one to itself.
All inputs are finite; a program needn't handle non-finite values.
Results may differ from a plain program's by a relative error of at most 0.03.
Values may be sent and summed in bfloat16 or wider, within the bound.
No kernel may reach another device: no remote copies, remote signals or barrier semaphores. Data moves between devices by JAX's collectives and lax.ppermute only.
A program may use at most 256 MiB of HBM per device.

v0:
```python
import functools
from types import SimpleNamespace as Bag

import jax
import jax.numpy as jnp
from jax import lax
from jax.experimental import pallas as pl
from jax.experimental.pallas import tpu as pltpu
from jax.sharding import PartitionSpec as P

F32 = jnp.float32
BF16 = jnp.bfloat16
I32 = jnp.int32

CHUNK = 4
TILE = 4
DP = "dp"
TENSOR = "tensor"
LATS = 6
HALF_COLS = 6
COST_CUT = 64
PARTS = 1
LN2 = 0.6931471805599453
NEVER = -1000000000.0
VMEM_LIMIT = 60 * 1024 * 1024


def mm(a, b):
    return lax.dot_general(a, b, (((1,), (0,)), ((), ())), preferred_element_type=F32)


def mm_nt(a, b):
    return lax.dot_general(a, b, (((1,), (1,)), ((), ())), preferred_element_type=F32)


def mm_tn(a, b):
    return lax.dot_general(a, b, (((0,), (0,)), ((), ())), preferred_element_type=F32)


def fold_rows(values):
    rows, width = values.shape
    return jnp.sum(values.reshape(rows // 8, 8, width), axis=0)


def plan_kernel(t_ref, mask_ref, next_ref, meta_ref, tab_ref, place_ref, seen, order, first, last, rows, cols):
    home = next_ref.shape[0]
    cap = tab_ref.shape[1]
    half = mask_ref.shape[1] // 2
    t = t_ref[0]

    def clear(s, carry):
        seen[s] = 0
        place_ref[0, s] = -1
        place_ref[1, s] = -1
        high = mask_ref[s, 0]
        for i in range(1, LATS):
            high += mask_ref[s, i * HALF_COLS]
        wide = mask_ref[s, 0] + mask_ref[s, half]
        for j in range(1, HALF_COLS):
            wide += mask_ref[s, j] + mask_ref[s, half + j]
        rows[s] = high
        cols[s] = wide
        return carry

    lax.fori_loop(0, home, clear, 0)

    def visit(origin, count):
        fresh = (rows[origin] > 0) & (seen[origin] == 0)

        def walk(carry):
            s, at, _ = carry
            seen[s] = 1
            order[at] = s
            first[at] = count
            following = next_ref[s]
            return following, at + 1, (following != origin) & (at + 1 < home)

        return lax.while_loop(lambda carry: carry[2], walk, (origin, count, fresh))[1]

    total = lax.fori_loop(0, home, visit, 0)

    def close(back, carry):
        p = total - 1 - back
        after = jnp.minimum(p + 1, home - 1)
        ends = (p == total - 1) | (first[after] != first[p])
        end = jnp.where(ends, p, carry)
        last[p] = end
        return end

    lax.fori_loop(0, total, close, 0)

    cut = (total + 1) // 2
    base = t * cut
    n = jnp.where(t == 0, cut, total - cut)

    def fill(i, carry):
        live = i < n
        p = jnp.where(live, base + i, 0)
        slot = jnp.where(live, order[p], 0)
        ahead = jnp.where(p == last[p], first[p], p + 1)
        behind = jnp.where(p == first[p], last[p], p - 1)
        next_slot = next_ref[slot]
        ahead_in = live & (ahead >= base) & (ahead < base + n)
        behind_in = live & (behind >= base) & (behind < base + n)
        tab_ref[0, i] = slot
        tab_ref[1, i] = jnp.where(ahead_in, ahead - base, -1)
        tab_ref[2, i] = jnp.where(behind_in, behind - base, -1)
        tab_ref[3, i] = jnp.where(live, rows[slot], 0)
        tab_ref[4, i] = jnp.where(live, cols[slot], 0)
        tab_ref[5, i] = jnp.where(live, rows[next_slot], 0)
        tab_ref[6, i] = jnp.where(live, cols[next_slot], 0)
        tab_ref[7, i] = jnp.where(live, next_slot, 0)
        return carry

    @pl.when(total == 0)
    def _():
        order[0] = 0
        first[0] = 0
        last[0] = 0

    lax.fori_loop(0, cap, fill, 0)

    def settle(p, carry):
        slot = order[p]
        owner = jnp.where(p >= cut, 1, 0)
        here = p - owner * cut
        source = jnp.where(owner == t, here, cap + here)
        place_ref[0, slot] = source
        place_ref[1, jnp.where(t == 1, slot, next_ref[slot])] = source
        return carry

    lax.fori_loop(0, total, settle, 0)

    crossing = (cut < total) & (first[jnp.minimum(cut, home - 1)] < cut)
    tail = jnp.maximum(cut - 1, 0)
    meta_ref[0] = n
    meta_ref[1] = jnp.where(crossing & (t == 0), first[jnp.minimum(cut, home - 1)], 0)
    meta_ref[2] = jnp.where(t == 0, tail, jnp.where(crossing, last[tail] - cut, 0))
    meta_ref[3] = t
    for spare in range(4, 8):
        meta_ref[spare] = 0


def make_plan(part, token_mask, shift_next, cap):
    home = shift_next.shape[0]
    smem = pl.BlockSpec(memory_space=pltpu.SMEM)
    return pl.pallas_call(
        plan_kernel,
        out_shape=(
            jax.ShapeDtypeStruct((8,), I32),
            jax.ShapeDtypeStruct((8, cap), I32),
            jax.ShapeDtypeStruct((2, home), I32),
        ),
        in_specs=[smem, smem, smem],
        out_specs=(smem, smem, smem),
        scratch_shapes=[pltpu.SMEM((home,), I32) for _ in range(6)],
        name="plan",
    )(part, token_mask, shift_next)


def gelu_pair(u):
    cdf = 0.5 + 0.5 * lax.erf(u * 0.7071067811865476)
    return u * cdf, cdf + u * (0.3989422804014327 * jnp.exp(-0.5 * (u * u)))


def normalise(values):
    centred = values - jnp.mean(values, axis=-1, keepdims=True)
    spread = jnp.mean(centred * centred, axis=-1, keepdims=True)
    scale = lax.rsqrt(spread + 1e-05)
    return centred * scale, scale


def norm_back(grad, unit, scale, gain):
    inner = grad * gain
    mean_one = jnp.mean(inner, axis=-1, keepdims=True)
    mean_two = jnp.mean(inner * unit, axis=-1, keepdims=True)
    return scale * (inner - mean_one - unit * mean_two)


def block_kernel(names, stages, index, head_width, span_of, *refs):
    ref = Bag(**dict(zip(names, refs, strict=True)))
    ahead, mixer, attention = stages
    if ahead or attention:
        in_sides = (ref.in_own, ref.in_oth)
    if ahead or mixer:
        out_sides, up_sides, down_sides = ((ref.out_own, ref.out_oth), (ref.up_own, ref.up_oth), (ref.down_own, ref.down_oth))
    if ahead:
        earth_sides, entry_sides = (ref.earth_own, ref.earth_oth), (ref.entry_own, ref.entry_oth)
        up_bias_sides = (ref.up_bias_own, ref.up_bias_oth)
    if mixer or attention:
        pack_sides = (ref.pack_own, ref.pack_oth)
    shifted = index == 1
    meta, tab = ref.meta, ref.tab
    cap = tab.shape[1]
    half, width = ref.xs.shape[2:]
    win = 2 * half
    rows_all = CHUNK * win
    part = width // 2
    groups = width // 128
    per_group = 128 // head_width
    heads = width // head_width
    own_heads = heads // 2
    scale = head_width**-0.5
    n = meta[0]
    t = meta[3]
    lead, span_count = span_of
    step = pl.program_id(0)
    w0 = lead + step * CHUNK
    first_step = step == 0
    lanes = lax.broadcasted_iota(I32, (1, 128), 1) // head_width
    head_keep = [jnp.where(lanes == k, 1.0, 0.0).astype(BF16) for k in range(per_group)]
    lane = lax.broadcasted_iota(I32, (win, 128), 1)
    spots = [((u + 1) % per_group) * head_width for u in range(per_group)]
    spare_lane = [lane == spot for spot in spots]
    spare_two = [(lane == spot) | (lane == spot + 1) for spot in spots]
    one = jnp.ones((), BF16)
    wide_step = TILE * win

    def row(table):
        return table[index : index + 1, :]

    def by_part(west, one_ref, other, at, dst, sem):
        is_own = t == (0 if west else 1)

        @pl.when(is_own)
        def _():
            pltpu.make_async_copy(one_ref.at[at], dst, sem).start()

        @pl.when(jnp.logical_not(is_own))
        def _():
            pltpu.make_async_copy(other.at[at], dst, sem).start()

    def by_place(local, local_half, one_ref, other, dst, sem):
        @pl.when(local >= 0)
        def _():
            pltpu.make_async_copy(one_ref.at[local, local_half], dst, sem).start()

        @pl.when(local < 0)
        def _():
            pltpu.make_async_copy(other, dst, sem).start()

    xs, x_sem = ref.xs, ref.x_sem
    if mixer:
        rs, r_sem = ref.rs, ref.r_sem

    if ahead:
        bias_copies = [
            pltpu.make_async_copy(
                side.at[index], ref.bias.at[pl.ds(s * own_heads, own_heads)], ref.b_sem.at[s]
            )
            for s, side in enumerate(earth_sides)
        ]

    @pl.when(first_step)
    def _():
        if ahead:
            for copy in bias_copies:
                copy.start()

        def start_loads(i, carry):
            if shifted:
                by_place(i, 1, ref.src, ref.src_oth, xs.at[i, 0], x_sem.at[i, 0])
                by_place(tab[1, i], 0, ref.src, ref.src_oth, xs.at[i, 1], x_sem.at[i, 1])
            else:
                by_part(True, ref.src, ref.src_oth, tab[0, i], xs.at[i, 0], x_sem.at[i, 0])
                by_part(False, ref.src, ref.src_oth, tab[0, i], xs.at[i, 1], x_sem.at[i, 1])
            if mixer and shifted:
                by_part(False, ref.grad_src, ref.grad_oth, tab[0, i], rs.at[i, 0], r_sem.at[i, 0])
                by_part(True, ref.grad_src, ref.grad_oth, tab[7, i], rs.at[i, 1], r_sem.at[i, 1])
            elif mixer:
                by_place(tab[2, i], 1, ref.grad_src, ref.grad_oth, rs.at[i, 0], r_sem.at[i, 0])
                by_place(i, 0, ref.grad_src, ref.grad_oth, rs.at[i, 1], r_sem.at[i, 1])
            return carry

        lax.fori_loop(lead, jnp.minimum(lead + span_count, n), start_loads, 0)

        def blank(i, carry):
            for k in range(2):
                xs[i, k] = jnp.zeros_like(xs[i, k])
                if mixer:
                    rs[i, k] = jnp.zeros_like(rs[i, k])
            return carry

        lax.fori_loop(jnp.maximum(n, lead), lead + span_count, blank, 0)
        if mixer:
            from_head = lax.broadcasted_iota(I32, (width, width), 0) // head_width
            to_head = lax.broadcasted_iota(I32, (width, width), 1) // head_width
            same = from_head // per_group == to_head // per_group
            following = (from_head + 1) % per_group == to_head % per_group
            ref.spread[...] = jnp.where(same & following, 1.0, 0.0).astype(BF16)
        if ahead or attention:
            for j in range(3):
                for s, side in enumerate(in_sides):
                    at = j * width + s * part
                    ref.w_in[at : at + part, :] = side[j]
        if ahead or mixer:
            for s, side in enumerate(out_sides):
                ref.wo[s * part : (s + 1) * part, :] = side[...]
            level = LATS * HALF_COLS
            place = lax.broadcasted_iota(I32, (win, 128), 0)
            inside = place
            for bound in (level, 2 * level, 3 * level):
                inside = inside - jnp.where(place >= bound, level, 0)
            lat = jnp.zeros_like(inside)
            for bound in range(HALF_COLS, level, HALF_COLS):
                lat = lat + jnp.where(inside >= bound, 1, 0)
            ref.lat[...] = lat
            ref.col[...] = inside - HALF_COLS * lat
        if ahead:
            for copy in bias_copies:
                copy.wait()
            for k in range(heads):
                ref.bias[k] = ref.bias[k] * (1.0 / LN2)
        sums = [ref.acc_small] if mixer or attention else []
        if mixer:
            sums += [ref.acc_up, ref.acc_down, ref.acc_hidden]
        if attention:
            sums += [ref.acc_in, ref.acc_out, ref.acc_earth, ref.acc_entry]
        for table in sums:
            table[...] = jnp.zeros_like(table)

    def extents(i):
        high, wide, high_next, wide_next = tab[3, i], tab[4, i], tab[5, i], tab[6, i]
        if shifted:
            return (high, wide - HALF_COLS), (high_next, wide_next)
        return (high, wide), (high, wide - HALF_COLS)

    def valid_rows(i, k):
        high, wide = extents(i)[k]
        valid = (ref.lat[:half] < high) & (ref.col[:half] < wide)
        return jnp.concatenate([jnp.where(valid, 1.0, 0.0)] * groups, axis=1)

    def tile_x(tile):
        parts = []
        for j in range(TILE):
            for k in range(2):
                parts.append(xs[w0 + tile * TILE + j, k].astype(F32))
        return jnp.concatenate(parts, axis=0)

    def entrance(tile, c):
        rows = pl.ds(pl.multiple_of(tile * wide_step, wide_step), wide_step)
        unit, _ = normalise(tile_x(tile))
        low = (unit * row(ref.gain_one) + row(ref.shift_one)).astype(BF16)
        ref.h1[rows, :] = low
        for j in range(3):
            cols = slice(j * width, (j + 1) * width)
            value = mm_nt(low, ref.w_in[cols, :])
            if j != 1:
                value = value + jnp.concatenate(
                    [side[index, j // 2 : j // 2 + 1, :] for side in entry_sides], axis=1
                )
            if j == 0:
                value = value * (scale / LN2)
            ref.qkv[rows, cols] = value.astype(BF16)
        return c

    def attend(pair, c):
        for j in range(2):
            attend_one(pair * 2 + j)
        return c

    def attend_one(w):
        rows = pl.ds(pl.multiple_of(w * win, win), win)
        (high_a, wide_a), (high_b, wide_b) = extents(w0 + w)
        west = lax.broadcasted_iota(I32, (win, 128), 0) < half
        high = jnp.where(west, high_a, high_b)
        wide = jnp.where(west, wide_a, wide_b)
        hide = jnp.where((ref.lat[...] < high) & (ref.col[...] < wide), 0.0, NEVER).astype(BF16)
        for g in range(groups):
            span = [slice(j * width + g * 128, j * width + (g + 1) * 128) for j in range(3)]
            q, k, v = (ref.qkv[rows, cols] for cols in span)
            total = None
            for u in range(per_group):
                head = g * per_group + u
                spare = spare_lane[u]
                s = mm_nt(jnp.where(spare, one, q * head_keep[u]), jnp.where(spare, hide, k))
                s = s + ref.bias[head]
                low = jnp.exp2(s - jnp.max(s, axis=-1, keepdims=True)).astype(BF16)
                ref.probs[w, head] = low
                keep = jnp.broadcast_to(head_keep[u], (win, 128))
                got = mm(low, jnp.concatenate([v * keep, keep], axis=1))
                total = got if total is None else total + got
            inverse = 1.0 / total[:, 128:]
            cols = slice(g * 128, (g + 1) * 128)
            ref.att[rows, cols] = (total[:, :128] * inverse).astype(BF16)
            ref.inverse[rows, cols] = inverse.astype(BF16)

    hidden_part = up_sides[0].shape[1] if ahead or mixer else 0
    hidden = 2 * hidden_part
    pieces = [(s, at) for s in range(2) for at in range(0, hidden_part, 384)]

    def middle(tile, c):
        rows = pl.ds(pl.multiple_of(tile * wide_step, wide_step), wide_step)
        att = ref.att[rows, :]
        v2 = tile_x(tile) + mm(att, ref.wo[...]) + row(ref.out_bias)
        unit, unit_scale = normalise(v2)
        if ahead:
            low = (unit * row(ref.gain_two) + row(ref.shift_two)).astype(BF16)
            ref.h2[rows, :] = low
            result = v2 + row(ref.down_bias)
        if mixer:
            parts = []
            for j in range(TILE):
                i = w0 + tile * TILE + j
                for k in range(2):
                    r = rs[i, k].astype(F32)
                    if shifted:
                        r = r * valid_rows(i, k)
                    parts.append(r)
            r = jnp.concatenate(parts, axis=0)
            r_low = r.astype(BF16)
            ref.rr[rows, :] = r_low
        d_h2 = None
        for s, off in pieces:
            cols = slice(off, off + 384)
            at = off + s * hidden_part
            span = slice(at, at + 384)
            if ahead:
                u = mm(low, up_sides[s][:, cols]) + up_bias_sides[s][index : index + 1, cols]
                g, slope = gelu_pair(u)
                g = g.astype(BF16)
                ref.act[rows, span] = g
                result = result + mm(g, down_sides[s][cols, :])
                if not mixer:
                    ref.slope[rows, span] = slope.astype(BF16)
            else:
                slope = ref.slope[rows, span].astype(F32)
            if mixer:
                du = mm_nt(r_low, down_sides[s][cols, :]) * slope
                ref.acc_hidden[:, span] += fold_rows(du)
                du = du.astype(BF16)
                ref.du[rows, span] = du
                d = mm_nt(du, up_sides[s][:, cols])
                d_h2 = d if d_h2 is None else d_h2 + d
        if ahead:
            for j in range(TILE):
                i = w0 + tile * TILE + j
                for k in range(2):
                    at = j * win + k * half
                    piece = result[at : at + half]
                    if not shifted:
                        ref.out[i, k] = piece.astype(BF16)
                        continue
                    piece = (piece * valid_rows(i, k)).astype(BF16)
                    place_half(ref.keep, ref.send, i, 1 - k, piece)
        if mixer:
            ref.acc_small[5] += fold_rows(r)
            ref.acc_small[4] += fold_rows(d_h2)
            ref.acc_small[3] += fold_rows(d_h2 * unit)
            dv2 = r + norm_back(d_h2, unit, unit_scale, row(ref.gain_two))
            ref.acc_small[2] += fold_rows(dv2)
            da = dv2.astype(BF16)
            ref.da[rows, :] = da
            d_att = mm_nt(da, ref.wo[...]) * ref.inverse[rows, :].astype(F32)
            ref.do[rows, :] = d_att.astype(BF16)
            inner = (d_att * att.astype(F32)).astype(BF16)
            delta = -mm(inner, ref.spread[...])
            high = delta.astype(BF16)
            rest = (delta - high.astype(F32)).astype(BF16)
            spot = lax.broadcasted_iota(I32, (1, width), 1) % head_width
            ref.aug[rows, :] = jnp.where(spot == 0, high, jnp.where(spot == 1, rest, jnp.zeros_like(rest)))
        return c

    def place_half(keep, send, i, owner, piece):
        @pl.when(t == owner)
        def _():
            keep[i] = piece

        @pl.when(t != owner)
        def _():
            send[i] = piece

    def hidden_grads(_, c):
        r_turned = ref.rr[...].T
        h_turned = ref.h2[...].T
        for at in range(0, hidden, 256):
            cols = slice(at, at + 256)
            ref.acc_down[:, cols] += mm(r_turned, ref.act[:, cols])
            ref.acc_up[:, cols] += mm(h_turned, ref.du[:, cols])
        return c

    def attend_back(pair, c):
        spans = [pl.ds(pl.multiple_of((pair * 2 + j) * win, win), win) for j in range(2)]
        for g in range(groups):
            span = [slice(j * width + g * 128, j * width + (g + 1) * 128) for j in range(3)]
            here = slice(g * 128, (g + 1) * 128)
            loaded = []
            for rows in spans:
                q, k, v = (ref.qkv[rows, cols] for cols in span)
                dog = ref.do[rows, here]
                loaded.append((q.T, k, v, dog, dog.T, ref.aug[rows, here], [], [], []))
            for u in range(per_group):
                head = g * per_group + u
                cut = slice(u * head_width, (u + 1) * head_width)
                total = None
                for j in range(2):
                    q_turned, k, v, dog, do_turned, augment, dq, dk, dv = loaded[j]
                    low = ref.probs[pair * 2 + j, head]
                    dom = jnp.where(spare_two[u], augment, dog * head_keep[u])
                    dp = mm_nt(dom, jnp.where(spare_two[u], one, v))
                    ds = low.astype(F32) * dp
                    total = ds if total is None else total + ds
                    ds = ds.astype(BF16)
                    dk.append(mm(q_turned[cut], ds))
                    dv.append(mm(do_turned[cut], low))
                    got = mm(ds, k * head_keep[u])
                    dq[:] = [got if not dq else dq[0] + got]
                ref.acc_earth[head] += total
            for j, rows in enumerate(spans):
                dq, dk, dv = loaded[j][6:]
                dq = dq[0] * scale
                dk = (jnp.concatenate(dk, axis=0) * LN2).T
                dv = jnp.concatenate(dv, axis=0).T
                for at, value in ((0, dq), (2, dv)):
                    ref.acc_entry[:, span[at]] += fold_rows(value)
                for at, value in enumerate((dq, dk, dv)):
                    ref.dqkv[rows, span[at]] = value.astype(BF16)
        return c

    def exit_back(tile, c):
        rows = pl.ds(pl.multiple_of(tile * wide_step, wide_step), wide_step)
        unit, unit_scale = normalise(tile_x(tile))
        dh = mm(ref.dqkv[rows, :], ref.w_in[...])
        ref.acc_small[1] += fold_rows(dh)
        ref.acc_small[0] += fold_rows(dh * unit)
        dv = ref.da[rows, :].astype(F32) + norm_back(dh, unit, unit_scale, row(ref.gain_one))
        for j in range(TILE):
            i = w0 + tile * TILE + j
            for k in range(2):
                at = j * win + k * half
                piece = dv[at : at + half].astype(BF16)
                if shifted:
                    ref.out[i, k] = piece
                else:
                    place_half(ref.keep, ref.send, i - lead, k, piece)
        return c

    def weight_grads(_, c):
        ref.acc_out[...] += mm(ref.att[...].T, ref.da[...])
        turned = ref.h1[...].T
        for j in range(3):
            cols = slice(j * width, (j + 1) * width)
            ref.acc_in[:, cols] += mm(turned, ref.dqkv[:, cols])
        return c

    @pl.when(w0 < n)
    def _():
        def wait_loads(i, c):
            for k in range(2):
                pltpu.make_async_copy(xs.at[i, k], xs.at[i, k], x_sem.at[i, k]).wait()
                if mixer:
                    pltpu.make_async_copy(rs.at[i, k], rs.at[i, k], r_sem.at[i, k]).wait()
            return c

        lax.fori_loop(w0, jnp.minimum(w0 + CHUNK, n), wait_loads, 0)
        if ahead:
            lax.fori_loop(0, CHUNK // TILE, entrance, 0)
            lax.fori_loop(0, CHUNK // 2, attend, 0)
        if ahead or mixer:
            lax.fori_loop(0, CHUNK // TILE, middle, 0)
        if mixer:
            lax.fori_loop(0, 1, hidden_grads, 0)
        if attention:
            lax.fori_loop(0, CHUNK // 2, attend_back, 0)
            lax.fori_loop(0, CHUNK // TILE, exit_back, 0)
            lax.fori_loop(0, 1, weight_grads, 0)

    @pl.when(step == pl.num_programs(0) - 1)
    def _():
        if ahead and not shifted:
            ref.out_half[...] = ref.out[meta[1], 0]
        if attention and shifted:
            ref.out_half[...] = ref.out[meta[2], 1]
        if mixer:
            for s, pack in enumerate(pack_sides):
                base = s * hidden_part
                for at in range(0, hidden_part, width):
                    cols = slice(base + at, base + at + width)
                    pack[at : at + width, :] = ref.acc_up[:, cols].astype(BF16)
                    pack[hidden_part + at : hidden_part + at + width, :] = ref.acc_down[:, cols].astype(BF16)
                if pack.shape[0] > 2 * hidden_part:
                    pack[2 * hidden_part :, :] = jnp.zeros_like(pack[2 * hidden_part :, :])
            ref.sums_small[...] = jnp.sum(ref.acc_small[...], axis=1)
            ref.sums_hidden[...] = jnp.sum(ref.acc_hidden[...], axis=0, keepdims=True)
        if attention:
            small = jnp.sum(ref.acc_small[...], axis=1)
            hidden_sum = ref.sums_hidden[...]
            if lead == 0:
                small = small + ref.sums_small[...]
            else:
                hidden_sum = jnp.zeros_like(hidden_sum)
            half_hidden = hidden_sum.shape[1] // 2
            entry_sum = jnp.sum(ref.acc_entry[...], axis=0, keepdims=True)
            layout = pack_rows(width, own_heads, win)
            for s, pack in enumerate(pack_sides):
                cuts = [slice(j * width + s * part, j * width + (s + 1) * part) for j in range(3)]
                for j, cut in enumerate(cuts):
                    at = layout.inward + j * part
                    pack[at : at + part, :] = ref.acc_in[:, cut].T.astype(BF16)
                pack[layout.out : layout.out + part, :] = ref.acc_out[s * part : (s + 1) * part, :].astype(BF16)
                earth = [ref.acc_earth[s * own_heads + k] for k in range(own_heads)]
                for k, value in enumerate(earth):
                    row_at = layout.earth + (k // 3) * win
                    pack[row_at : row_at + win, (k % 3) * 128 : (k % 3 + 1) * 128] = value[:, :128].astype(BF16)
                rest = jnp.concatenate([value[:, 128:] for value in earth], axis=1)
                rest = jnp.concatenate([rest, jnp.zeros((win, 128 - rest.shape[1]), F32)], axis=1)
                third = win // 3
                for k in range(3):
                    pack[layout.rest : layout.rest + third, k * 128 : (k + 1) * 128] = rest[
                        k * third : (k + 1) * third
                    ].astype(BF16)
                lines = [small]
                for at in range(s * half_hidden, (s + 1) * half_hidden, width):
                    lines.append(hidden_sum[:, at : at + width])
                lines.append(jnp.concatenate([entry_sum[:, cuts[0]], entry_sum[:, cuts[2]]], axis=1))
                count = small.shape[0] + len(lines) - 1
                lines.append(jnp.zeros((16 - count, width), F32))
                pack[layout.small : layout.small + 16, :] = jnp.concatenate(lines, axis=0).astype(BF16)
                if pack.shape[0] > layout.total:
                    pack[layout.total :, :] = jnp.zeros_like(pack[layout.total :, :])


def pack_rows(width, own_heads, win):
    counts = dict(
        inward=3 * width // 2, out=width // 2, earth=own_heads // 3 * win, rest=win // 3, small=16, total=0
    )
    layout, at = {}, 0
    for name, count in counts.items():
        layout[name] = at
        at += count
    return Bag(**layout)


def padded(rows, devices):
    unit = 16 * devices
    return -(-rows // unit) * unit


def run_block(stages, index, given, sizes, devices, split):
    cap, half, width, own_heads, hidden_part = sizes
    ahead, mixer, attention = stages
    shifted = index == 1
    win = 2 * half
    rows = CHUNK * win
    heads = 2 * own_heads
    hidden = 2 * hidden_part
    head_width = width // heads
    which, parts = split
    steps = cap // CHUNK // parts
    lead = which * steps * CHUNK
    smem = pl.BlockSpec(memory_space=pltpu.SMEM)
    hbm = pl.BlockSpec(memory_space=pl.ANY)
    ins, outs, scratch = {}, {}, {}

    def whole(shape):
        zeros = (0,) * len(shape)
        return pl.BlockSpec(shape, lambda c: zeros, pipeline_mode=pl.Buffered(1))

    def take(spec, **arrays):
        for name, array in arrays.items():
            ins[name] = (array, whole(array.shape) if spec is None else spec)

    def take_block(**arrays):
        for name, array in arrays.items():
            at = (index,) + (0,) * (array.ndim - 1)
            spec = pl.BlockSpec((None,) + array.shape[1:], lambda c, at=at: at, pipeline_mode=pl.Buffered(1))
            ins[name] = (array, spec)

    def chunked(shape):
        zeros = (0,) * (len(shape) - 1)
        return pl.BlockSpec(shape, lambda c: (which * steps + c,) + zeros)

    def give(dtype=BF16, **shapes):
        for name, shape in shapes.items():
            outs[name] = (jax.ShapeDtypeStruct(shape, dtype), whole(shape))

    flat = lambda factor: (rows, factor * width)
    stash = dict(
        qkv=flat(3),
        probs=(CHUNK, heads, win, win),
        att=flat(1),
        inverse=flat(1),
        h1=flat(1),
        h2=flat(1),
        act=(rows, hidden),
        slope=(rows, hidden),
        da=flat(1),
        do=flat(1),
        aug=flat(1),
    )

    def carry_in(**arrays):
        for name, array in arrays.items():
            ins[name] = (array, chunked(stash[name]))

    def carry_out(**wanted):
        for name in wanted:
            shape = stash[name]
            full = jax.ShapeDtypeStruct((shape[0] * cap // CHUNK,) + shape[1:], BF16)
            outs[name] = (full, chunked(shape))

    g = given
    take(smem, meta=g.meta, tab=g.tab)
    take(hbm, src=g.src, src_oth=g.src_oth)
    if mixer:
        take(hbm, grad_src=g.grad_src, grad_oth=g.grad_oth)
    if ahead:
        take(hbm, earth_own=g.earth_own, earth_oth=g.earth_oth)
        take(None, shift_one=g.shift_one, shift_two=g.shift_two, down_bias=g.down_bias)
        take(None, entry_own=g.entry_own, entry_oth=g.entry_oth)
        take(None, up_bias_own=g.up_bias_own, up_bias_oth=g.up_bias_oth)
    if ahead or mixer:
        take(None, out_bias=g.out_bias, gain_two=g.gain_two)
        take_block(out_own=g.out_own, out_oth=g.out_oth, up_own=g.up_own, up_oth=g.up_oth)
        take_block(down_own=g.down_own, down_oth=g.down_oth)
    if ahead or attention:
        take(None, gain_one=g.gain_one)
        take_block(in_own=g.in_own, in_oth=g.in_oth)
    if attention:
        take(None, sums_small=g.sums_small, sums_hidden=g.sums_hidden)
        carry_in(qkv=g.qkv, probs=g.probs, att=g.att, h1=g.h1, da=g.da, do=g.do, aug=g.aug)
    elif not ahead:
        carry_in(att=g.att, inverse=g.inverse, h2=g.h2, act=g.act, slope=g.slope)

    half_shape = (half, width)
    if ahead:
        carry_out(qkv=1, probs=1, att=1, h1=1)
        if not mixer:
            carry_out(inverse=1, h2=1, act=1, slope=1)
    if mixer:
        carry_out(da=1, do=1, aug=1)
    if (ahead and not shifted) or (attention and shifted):
        give(out=(cap, 2) + half_shape, out_half=half_shape)
    if (ahead and shifted) or (attention and not shifted):
        give(keep=(cap // parts,) + half_shape, send=(cap // parts,) + half_shape)
    if mixer:
        pack = (padded(2 * hidden_part, devices), width)
        give(pack_own=pack, pack_oth=pack)
        give(F32, sums_small=(6, width), sums_hidden=(1, hidden))
    if attention:
        pack = (padded(pack_rows(width, own_heads, win).total, devices), width)
        give(pack_own=pack, pack_oth=pack)

    def hold(dtype=BF16, **shapes):
        for name, shape in shapes.items():
            scratch[name] = pltpu.VMEM(shape, dtype)

    halves = (cap, 2) + half_shape
    hold(xs=halves)
    scratch.update(x_sem=pltpu.SemaphoreType.DMA((cap, 2)))
    if ahead:
        hold(F32, bias=(heads, win, win))
        scratch.update(b_sem=pltpu.SemaphoreType.DMA((2,)))
    if ahead or attention:
        hold(w_in=(3 * width, width))
    if ahead or mixer:
        hold(wo=(width, width))
        hold(I32, lat=(win, 128), col=(win, 128))
    if ahead and mixer:
        hold(inverse=flat(1), h2=flat(1), act=(rows, hidden))
    if mixer:
        hold(rs=halves, rr=flat(1), du=(rows, hidden), spread=(width, width))
        scratch.update(r_sem=pltpu.SemaphoreType.DMA((cap, 2)))
        hold(F32, acc_up=(width, hidden), acc_down=(width, hidden), acc_hidden=(8, hidden))
    if attention:
        hold(dqkv=flat(3))
        hold(F32, acc_in=(width, 3 * width), acc_out=(width, width))
        hold(F32, acc_earth=(heads, win, win), acc_entry=(8, 3 * width))
    if mixer or attention:
        hold(F32, acc_small=(6, 8, width))

    matmuls = cap * win * (4 * width * width + 2 * width * hidden)
    result = pl.pallas_call(
        functools.partial(
            block_kernel, [*ins, *outs, *scratch], stages, index, head_width, (lead, steps * CHUNK)
        ),
        grid=(steps,),
        out_shape=tuple(shape for shape, _ in outs.values()),
        in_specs=[spec for _, spec in ins.values()],
        out_specs=tuple(spec for _, spec in outs.values()),
        scratch_shapes=list(scratch.values()),
        compiler_params=pltpu.CompilerParams(vmem_limit_bytes=VMEM_LIMIT),
        cost_estimate=pl.CostEstimate(
            flops=2 * sum(stages) * matmuls // COST_CUT,
            bytes_accessed=8 * sum(stages) * cap * win * width * 2 // COST_CUT,
            transcendentals=cap * win * hidden // COST_CUT,
        ),
        name=("ahead" if ahead else "") + ("mixer" if mixer else "") + ("attention" if attention else "") + str(index + 1),
    )(*(array for array, _ in ins.values()))
    return Bag(**dict(zip(outs, result, strict=True)))


def settle_kernel(counts, place, *refs):
    refs = list(refs)
    held = [[refs.pop(0) for _ in range(count)] for count in counts]
    out_a, out_b, zeros, sems = refs
    home = place.shape[1]
    zeros[...] = jnp.zeros_like(zeros)

    def start(s, carry):
        for j, out in enumerate((out_a, out_b)):
            source = place[j, s]

            @pl.when(source < 0)
            def _(out=out, j=j):
                pltpu.make_async_copy(zeros, out.at[s], sems.at[j, s]).start()

            low = 0
            for ref in held[j]:
                high = low + ref.shape[0]

                @pl.when((source >= low) & (source < high))
                def _(ref=ref, out=out, j=j, at=source - low):
                    pltpu.make_async_copy(ref.at[at], out.at[s], sems.at[j, s]).start()

                low = high

        return carry

    lax.fori_loop(0, home, start, 0)

    def finish(s, carry):
        for j, out in enumerate((out_a, out_b)):
            pltpu.make_async_copy(zeros, out.at[s], sems.at[j, s]).wait()
        return carry

    lax.fori_loop(0, home, finish, 0)


def settle(place, first, second):
    home = place.shape[1]
    half_shape = first[0].shape[1:]
    hbm = pl.BlockSpec(memory_space=pl.ANY)
    vmem = pl.BlockSpec(memory_space=pltpu.VMEM)
    shape = jax.ShapeDtypeStruct((home,) + half_shape, BF16)
    counts = (len(first), len(second))
    return pl.pallas_call(
        functools.partial(settle_kernel, counts),
        out_shape=(shape, shape),
        in_specs=[pl.BlockSpec(memory_space=pltpu.SMEM)] + [vmem] * sum(counts),
        out_specs=(hbm, hbm),
        scratch_shapes=[pltpu.VMEM(half_shape, BF16), pltpu.SemaphoreType.DMA((2, home))],
        compiler_params=pltpu.CompilerParams(vmem_limit_bytes=VMEM_LIMIT),
        name="settle",
    )(place, *first, *second)


def local_kernel(jobs, digits_ref, *refs):
    refs = list(refs)
    ins = [[refs.pop(0) for _ in range(count)] for _, count, _, _ in jobs]
    outs = [[refs.pop(0) for _ in range(size if scatter else 1)] for scatter, _, size, _ in jobs]
    assert not refs
    for (scatter, _, size, stage), parts, made in zip(jobs, ins, outs):
        digit = digits_ref[stage]
        if scatter:
            rows = made[0].shape[0]
            for k, out in enumerate(made):
                at = pl.multiple_of((digit ^ k) * rows, rows) if size > 1 else 0
                total = parts[0][pl.ds(at, rows), :].astype(F32)
                for part in parts[1:]:
                    total = total + part[pl.ds(at, rows), :].astype(F32)
                out[...] = total.astype(BF16)
        else:
            rows = parts[0].shape[0]
            for k, part in enumerate(parts):
                made[0][pl.ds(pl.multiple_of((digit ^ k) * rows, rows), rows), :] = part[...]


def dp_groups(devices):
    sizes = []
    while devices > 1:
        size = 4 if devices % 4 == 0 else 2
        sizes.append(size)
        devices //= size
    return sizes


def with_peer(value, stride, k):
    devices = lax.axis_size(DP)
    return lax.ppermute(value, DP, [(d, d ^ (k * stride)) for d in range(devices)])


def stack_kernel(*refs):
    out, pairs = refs[-1], refs[:-1]
    at = 0
    for one, other in zip(pairs[0::2], pairs[1::2]):
        rows = one.shape[0]
        out[at : at + rows, :] = (one[...].astype(F32) + other[...].astype(F32)).astype(BF16)
        at += rows


def stack(*pairs):
    vmem = pl.BlockSpec(memory_space=pltpu.VMEM)
    rows = sum(pair[0].shape[0] for pair in pairs)
    return pl.pallas_call(
        stack_kernel,
        out_shape=jax.ShapeDtypeStruct((rows, pairs[0][0].shape[1]), BF16),
        in_specs=[vmem] * (2 * len(pairs)),
        out_specs=vmem,
        compiler_params=pltpu.CompilerParams(vmem_limit_bytes=VMEM_LIMIT),
        name="stack",
    )(*(value for pair in pairs for value in pair))


class DpSum:
    def __init__(self, parts):
        self.parts = parts
        self.phase = 0
        self.stages, stride = [], 1
        for size in dp_groups(lax.axis_size(DP)):
            self.stages.append((size, stride))
            stride *= size

    def job(self):
        count = len(self.stages)
        if self.phase < count:
            return (True, len(self.parts), self.stages[self.phase][0], self.phase)
        if self.phase == count:
            return (True, len(self.parts), 1, 0)
        stage = 2 * count - self.phase
        return (False, len(self.parts), self.stages[stage][0], stage)

    def accept(self, made):
        count = len(self.stages)
        if self.phase < count:
            size, stride = self.stages[self.phase]
            self.parts = [made[0]] + [with_peer(made[k], stride, k) for k in range(1, size)]
        elif self.phase < 2 * count:
            size, stride = self.stages[2 * count - 1 - self.phase]
            self.parts = [made[0]] + [with_peer(made[0], stride, k) for k in range(1, size)]
        else:
            self.parts = made
        self.phase += 1

    def last(self):
        return self.phase >= 2 * len(self.stages)


def advance(sums, digits, *ties):
    sums = [s for s in sums if not s.last()]
    if not sums:
        return ties
    jobs = [s.job() for s in sums]
    inputs, shapes, counts = [], [], []
    for s, (scatter, count, size, _) in zip(sums, jobs):
        rows, width = s.parts[0].shape
        inputs += s.parts
        made = [(rows // size, width)] * size if scatter else [(rows * size, width)]
        shapes += made
        counts.append(len(made))
    smem = pl.BlockSpec(memory_space=pltpu.SMEM)
    vmem = pl.BlockSpec(memory_space=pltpu.VMEM)
    outs = pl.pallas_call(
        functools.partial(local_kernel, jobs),
        out_shape=tuple(jax.ShapeDtypeStruct(shape, BF16) for shape in shapes),
        in_specs=[smem] + [vmem] * len(inputs),
        out_specs=(vmem,) * len(shapes),
        compiler_params=pltpu.CompilerParams(vmem_limit_bytes=VMEM_LIMIT),
        name="fold",
    )(digits, *inputs)
    outs, ties = lax.optimization_barrier((list(outs), ties))
    for s, count in zip(sums, counts):
        s.accept(outs[:count])
        outs = outs[count:]
    return ties


def unpack_kernel(layout, count, digit_ref, *refs):
    refs = list(refs)
    pieces = [[refs.pop(0) for _ in range(count)] for _ in range(2)]
    whole_two = refs.pop(0)
    up, down, inward, out, earth, small, hidden, entry, *joined = refs
    digit = digit_ref[0]
    for parts, whole in zip(pieces, joined):
        rows = parts[0].shape[0]
        for k, piece in enumerate(parts):
            whole[pl.ds(pl.multiple_of((digit ^ k) * rows, rows), rows), :] = piece[...]
    width = up.shape[1]
    hidden_part = up.shape[2]
    part = width // 2
    win = earth.shape[2]
    third = win // 3
    split = joined[0].shape[0]
    packs = [(joined[0], 0, joined[1], 0), (whole_two, 0, whole_two, split)]
    for b, (pack, base, other, base_other) in enumerate(packs):
        for at in range(0, hidden_part, width):
            low = base + at
            up[b, :, at : at + width] = pack[low : low + width, :].astype(F32)
            low += hidden_part
            down[b, at : at + width, :] = pack[low : low + width, :].T.astype(F32)

        def lines_of(place, start, size):
            low = base_other + place + start
            return other[low : low + size, :].astype(F32)

        for j in range(3):
            inward[b, j] = lines_of(layout.inward, j * part, part)
        out[b] = lines_of(layout.out, 0, part)
        rest = lines_of(layout.rest, 0, third)
        rest = jnp.concatenate([rest[:, k * 128 : (k + 1) * 128] for k in range(3)], axis=0)
        for k in range(earth.shape[1]):
            main = lines_of(layout.earth, (k // 3) * win, win)
            earth[b, k, :, :128] = main[:, (k % 3) * 128 : (k % 3 + 1) * 128]
            earth[b, k, :, 128:] = rest[:, k * (win - 128) : (k + 1) * (win - 128)]
        lines = lines_of(layout.small, 0, 16)
        small[b] = lines[:6]
        for j, at in enumerate(range(0, hidden_part, width)):
            hidden[b : b + 1, at : at + width] = lines[6 + j : 7 + j]
        last = lines[6 + hidden_part // width : 7 + hidden_part // width]
        entry[b, 0:1] = last[:, :part]
        entry[b, 1:2] = last[:, part:]


def unpack(digit, hidden_parts, attention_parts, whole_two, width, hidden_part, own_heads, win):
    vmem = pl.BlockSpec(memory_space=pltpu.VMEM)
    shapes = (
        (2, width, hidden_part),
        (2, hidden_part, width),
        (2, 3, width // 2, width),
        (2, width // 2, width),
        (2, own_heads, win, win),
        (2, 6, width),
        (2, hidden_part),
        (2, 2, width // 2),
    )
    count = len(hidden_parts)
    return pl.pallas_call(
        functools.partial(unpack_kernel, pack_rows(width, own_heads, win), count),
        out_shape=tuple(jax.ShapeDtypeStruct(shape, F32) for shape in shapes),
        in_specs=[pl.BlockSpec(memory_space=pltpu.SMEM)] + [vmem] * (2 * count + 1),
        out_specs=(vmem,) * len(shapes),
        scratch_shapes=[
            pltpu.VMEM((parts[0].shape[0] * count, width), BF16) for parts in (hidden_parts, attention_parts)
        ],
        compiler_params=pltpu.CompilerParams(vmem_limit_bytes=VMEM_LIMIT),
        name="unpack",
    )(digit, *hidden_parts, *attention_parts, whole_two)


def across(value):
    return lax.ppermute(value, TENSOR, [(0, 1), (1, 0)])


def local(
    tokens,
    token_mask,
    shift_next,
    cotangent,
    attend_gain,
    attend_shift,
    inward_weight,
    inward_bias,
    earth_bias,
    outward_weight,
    outward_bias,
    mixer_gain,
    mixer_shift,
    up_weight,
    up_bias,
    down_weight,
    down_bias,
):
    home, half, width = tokens.shape
    cap = home // 2
    part = lax.axis_index(TENSOR).astype(I32).reshape(1)
    tokens_oth = across(tokens)
    inward = jnp.transpose(inward_weight, (0, 2, 3, 1))
    own_heads = earth_bias.shape[1]
    hidden_part = up_weight.shape[2]
    win = 2 * half
    cotangent_oth = across(cotangent)
    meta, tab, place = make_plan(part, token_mask, shift_next, cap)
    common = dict(
        meta=meta,
        tab=tab,
        gain_one=attend_gain,
        shift_one=attend_shift,
        out_bias=outward_bias,
        gain_two=mixer_gain,
        shift_two=mixer_shift,
        down_bias=down_bias,
        entry_own=inward_bias,
        entry_oth=across(inward_bias),
        up_bias_own=up_bias,
        up_bias_oth=across(up_bias),
        in_own=inward,
        in_oth=across(inward),
        earth_own=earth_bias,
        earth_oth=across(earth_bias),
        out_own=outward_weight,
        out_oth=across(outward_weight),
        up_own=up_weight,
        up_oth=across(up_weight),
        down_own=down_weight,
        down_oth=across(down_weight),
    )
    sizes = (cap, half, width, own_heads, hidden_part)
    devices = lax.axis_size(DP)

    def run(stages, index, *more, split=(0, 1)):
        given = dict(common)
        for group in more:
            given.update(vars(group))
        return run_block(stages, index, Bag(**given), sizes, devices, split)

    rank = lax.axis_index(DP).astype(I32)
    digits, stride = [], 1
    for size in dp_groups(devices):
        digits.append(rank // stride % size)
        stride *= size
    digits = jnp.stack(digits)

    def sum_of(kernel):
        return DpSum([kernel.pack_own, across(kernel.pack_oth)])

    first = Bag(src=tokens, src_oth=tokens_oth)
    ahead_one = run((True, False, False), 0, first)
    second = Bag(src=ahead_one.out, src_oth=across(ahead_one.out_half))
    mixer_two = run((True, True, False), 1, second, Bag(grad_src=cotangent, grad_oth=cotangent_oth))
    pack_far = across(mixer_two.pack_oth)
    recv_b = across(mixer_two.send)
    attention_two = run((False, False, True), 1, mixer_two, second)
    half_far = across(attention_two.out_half)
    pack_two = stack((mixer_two.pack_own, pack_far), (attention_two.pack_own, across(attention_two.pack_oth)))
    pack_two, half_far = lax.optimization_barrier((pack_two, half_far))
    sum_two = lax.psum(pack_two, DP)
    back = Bag(grad_src=attention_two.out, grad_oth=half_far)
    mixer_one = run((False, True, False), 0, ahead_one, first, back)
    sum_mixer_one = sum_of(mixer_one)
    (do,) = advance([sum_mixer_one], digits, mixer_one.do)
    halves, across_one = [], []
    for which in range(PARTS):
        if which:
            (do,) = advance([sum_mixer_one], digits, do)
        halves.append(run((False, False, True), 0, ahead_one, mixer_one, Bag(do=do), first, split=(which, PARTS)))
        across_one.append(across(halves[-1].pack_oth))
    sum_attention_one = DpSum([half_of.pack_own for half_of in halves] + across_one)
    recv_a = [across(half_of.send) for half_of in halves]
    sums = [sum_mixer_one, sum_attention_one]
    while not all(s.last() for s in sums):
        advance(sums, digits)
    tokens_grad, block_output = settle(
        place, [half_of.keep for half_of in halves] + recv_a, [mixer_two.keep, recv_b]
    )
    g_up, g_down, g_in, g_out, g_earth, small, hidden, entry = unpack(
        digits[:1], sum_mixer_one.parts, sum_attention_one.parts, sum_two, width, hidden_part, own_heads, win
    )
    return (
        block_output,
        tokens_grad,
        small[:, 0],
        small[:, 1],
        jnp.transpose(g_in, (0, 3, 1, 2)),
        entry,
        g_earth,
        g_out,
        small[:, 2],
        small[:, 3],
        small[:, 4],
        g_up,
        hidden,
        g_down,
        small[:, 5],
    )


def solution(mesh):
    placed = (
        P(DP, TENSOR, None),
        P(DP, None),
        P(DP),
        P(DP, TENSOR, None),
        P(),
        P(),
        P(None, None, None, TENSOR),
        P(None, None, TENSOR),
        P(None, TENSOR, None, None),
        P(None, TENSOR, None),
        P(),
        P(),
        P(),
        P(None, None, TENSOR),
        P(None, TENSOR),
        P(None, TENSOR, None),
        P(),
    )
    return jax.shard_map(
        local,
        mesh=mesh,
        in_specs=placed,
        out_specs=(
            P(DP, TENSOR, None),
            P(DP, TENSOR, None),
            P(),
            P(),
            P(None, None, None, TENSOR),
            P(None, None, TENSOR),
            P(None, TENSOR, None, None),
            P(None, TENSOR, None),
            P(),
            P(),
            P(),
            P(None, None, TENSOR),
            P(None, TENSOR),
            P(None, TENSOR, None),
            P(),
        ),
        check_vma=False,
    )
```

profile of v0, /device:TPU:0, one launch (start us, length us, event | category | flops | bytes accessed | tf_op | source)
XLA Modules:
  0.0 386.8 jit_solution(303453014490569976)
XLA Ops:
  8.8 6.7 %collective-permute-done.3.refs_10_.refs_12_ = f32[2,2,192]{2,1,0:T(2,128)S(1)} collective-permute-done((f32[2,2,192]{2,1,0:T(2,128)}, f32[2,2,192]{2,1,0:T(2,128)S(1)}, u32[]{:S(2)}, u32[]{:S(2)}) %collective-permute-start.3) | collective-permute-done | bytes 3104 | tf_op jit(solution)/shard_map/ppermute | solution.py:1041
  15.9 1.0 collective-permute-done.4.refs_12_.refs_14_
  17.8 4.1 %plan.1 = (s32[8]{0:T(128)}, s32[8,16]{1,0:T(8,128)}, s32[2,32]{1,0:T(2,128)}) custom-call(s32[1]{0:T(128)} %bitcast.t_ref, s32[32,144]{1,0:T(8,128)} %mask_ref.1, s32[32]{0:T(128)} %next_ref.1), custom_call_target="tpu_custom_call" | custom-call | tf_op jit(solution)/shard_map/plan/pallas_call | solution.py:147
  21.9 2.4 collective-permute-done.2.refs_5_.refs_7_
  24.4 1.2 copy-done
  25.5 36.6 %ahead1.1 = (bf16[2304,1152]{1,0:T(8,128)(2,1)}, bf16[16,12,144,144]{3,2,1,0:T(8,128)(2,1)}, bf16[2304,384]{1,0:T(8,128)(2,1)}, bf16[2304,384]{1,0:T(8,128)(2,1)...) custom-call(s32[8]{0:T(128)} %get-tuple-element.93.refs_0_, ...), custom_call_target="tpu_custom_call" | custom-call | flops 127401984 | bytes 221184 | tf_op jit(solution)/shard_map/ahead1/pallas_call | solution.py:773
  62.5 1.1 collective-permute-done.8.refs_3_
  64.3 51.4 %aheadmixer2.1 = (bf16[2304,1152]{1,0:T(8,128)(2,1)}, bf16[16,12,144,144]{3,2,1,0:T(8,128)(2,1)}, bf16[2304,384]{1,0:T(8,128)(2,1)}, bf16[2304,384]{1,0:T(8,128)...) custom-call(s32[8]{0:T(128)} %get-tuple-element.93.refs_0_, ...), custom_call_target="tpu_custom_call" | custom-call | flops 254803968 | bytes 442368 | tf_op jit(solution)/shard_map/aheadmixer2/pallas_call | solution.py:773
  116.1 34.7 %attention2.1 = (bf16[16,2,72,384]{3,2,1,0:T(8,128)(2,1)}, bf16[72,384]{1,0:T(8,128)(2,1)}, bf16[1280,384]{1,0:T(8,128)(2,1)}, bf16[1280,384]{1,0:T(8,128)(2,1)}) custom-call(s32[8]{0:T(128)} %get-tuple-element.93.refs_0_, s32[8,16]{1,0:T(8,128)} %get-tuple-element.94.refs_1_, bf16[16,2,72,384]{3,2,1,0:T(8,128)(2,1)} %get-tuple-element.95.refs_2_, ...), custom_call_target="tpu_custom_call" | custom-call | flops 127401984 | bytes 221184 | tf_op jit(solution)/shard_map/attention2/pallas_call | solution.py:773
  151.4 2.3 collective-permute-done.11.refs_3_
  153.7 1.0 copy-done.5
  155.0 4.1 %stack.13 = bf16[2816,384]{1,0:T(8,128)(2,1)} custom-call(bf16[1536,384]{1,0:T(8,128)(2,1)} %get-tuple-element.107.refs_0_, bf16[1536,384]{1,0:T(8,128)(2,1)} %copy-done.3, bf16[1280,384]{1,0:T(8,128)(2,1)} %get-tuple-element.109.refs_2_, bf16[1280,384]{1,0:T(8,128)(2,1)} %copy-done.5), custom_call_target="tpu_custom_call" | custom-call | tf_op jit(solution)/shard_map/stack/pallas_call | solution.py:895
  159.7 24.9 %mixer1.1 = (bf16[2304,384]{1,0:T(8,128)(2,1)}, bf16[2304,384]{1,0:T(8,128)(2,1)}, bf16[2304,384]{1,0:T(8,128)(2,1)}, bf16[1536,384]{1,0:T(8,128)(2,1)}, bf16[15...) custom-call(s32[8]{0:T(128)} %get-tuple-element.93.refs_0_, s32[8,16]{1,0:T(8,128)} %get-tuple-element.94.refs_1_, ...), custom_call_target="tpu_custom_call" | custom-call | flops 127401984 | bytes 221184 | tf_op jit(solution)/shard_map/mixer1/pallas_call | solution.py:773
  185.5 2.2 collective-permute-done.13.refs_1_
  187.7 1.0 copy-done.4
  188.7 2.7 fold.5
  191.4 36.1 %attention1.1 = (bf16[16,72,384]{2,1,0:T(8,128)(2,1)}, bf16[16,72,384]{2,1,0:T(8,128)(2,1)}, bf16[1280,384]{1,0:T(8,128)(2,1)}, bf16[1280,384]{1,0:T(8,128)(2,1)}) custom-call(s32[8]{0:T(128)} %get-tuple-element.93.refs_0_, s32[8,16]{1,0:T(8,128)} %get-tuple-element.94.refs_1_, bf16[32,72,384]{2,1,0:T(8,128)(2,1)} %refs_2_.5, bf16[32,72,384]{2,1,0:T(8,128)(2,1)} %copy-done, ...), custom_call_target="tpu_custom_call" | custom-call | flops 127401984 | bytes 221184 | tf_op jit(solution)/shard_map/attention1/pallas_call | solution.py:773
  227.8 44.5 %collective-permute-start.17 = (bf16[384,384]{1,0:T(8,128)(2,1)}, bf16[384,384]{1,0:T(8,128)(2,1)S(1)}, u32[]{:S(2)}, u32[]{:S(2)}) collective-permute-start(bf16[384,384]{1,0:T(8,128)(2,1)} %get-tuple-element.141), channel_id=1, source_target_pairs={{0,4},{2,6},{4,0},{6,2},{8,12},{10,14},{12,8},{14,10},{16,20},{18,... | collective-permute-start | bytes 884744 | tf_op jit(solution)/shard_map/ppermute | solution.py:880
  272.8 13.1 %collective-permute-done.17.refs_2_ = bf16[384,384]{1,0:T(8,128)(2,1)S(1)} collective-permute-done((bf16[384,384]{1,0:T(8,128)(2,1)}, bf16[384,384]{1,0:T(8,128)(2,1)S(1)}, u32[]{:S(2)}, u32[]{:S(2)}) %collective-permute-start.17) | collective-permute-done | bytes 294944 | tf_op jit(solution)/shard_map/ppermute | solution.py:880
  287.0 3.1 fold.6
  290.1 1.8 collective-permute-start.20
  291.9 2.4 collective-permute-start.21
  294.5 0.9 collective-permute-done.20.refs_1_
  295.4 2.2 collective-permute-start.23
  297.5 3.3 collective-permute-done.21.refs_2_
  301.7 1.3 collective-permute-start.25
  303.0 11.1 %collective-permute-done.24.refs_6_ = bf16[320,384]{1,0:T(8,128)(2,1)S(1)} collective-permute-done((bf16[320,384]{1,0:T(8,128)(2,1)}, bf16[320,384]{1,0:T(8,128)(2,1)S(1)}, u32[]{:S(2)}, u32[]{:S(2)}) %collective-permute-start.24) | collective-permute-done | bytes 245792 | tf_op jit(solution)/shard_map/ppermute | solution.py:880
  314.9 2.2 fold.7
  317.1 2.8 collective-permute-start.30
  319.9 1.6 collective-permute-start.31
  322.4 3.1 collective-permute-start.27
  326.3 1.9 collective-permute-start.28
  328.3 5.9 %collective-permute-done.28.refs_3_ = bf16[96,384]{1,0:T(8,128)(2,1)S(1)} collective-permute-done((bf16[96,384]{1,0:T(8,128)(2,1)}, bf16[96,384]{1,0:T(8,128)(2,1)S(1)}, u32[]{:S(2)}, u32[]{:S(2)}) %collective-permute-start.28) | collective-permute-done | bytes 73760 | tf_op jit(solution)/shard_map/ppermute | solution.py:880
  334.8 1.8 fold.8
  336.7 6.2 %collective-permute-start.35 = (bf16[80,384]{1,0:T(8,128)(2,1)}, bf16[80,384]{1,0:T(8,128)(2,1)S(1)}, u32[]{:S(2)}, u32[]{:S(2)}) collective-permute-start(bf16[80,384]{1,0:T(8,128)(2,1)} %get-tuple-element.159.refs_0_), channel_id=1, source_target_pairs={{0,8},{2,10},{4,12},{6,14},{8,0},{10,2},{12,4},{14,6},{16,24},{18,... | collective-permute-start | bytes 184328 | tf_op jit(solution)/shard_map/ppermute | solution.py:880
  342.8 4.5 %collective-permute-start.36 = (bf16[80,384]{1,0:T(8,128)(2,1)}, bf16[80,384]{1,0:T(8,128)(2,1)S(1)}, u32[]{:S(2)}, u32[]{:S(2)}) collective-permute-start(bf16[80,384]{1,0:T(8,128)(2,1)} %get-tuple-element.159.refs_0_), channel_id=1, source_target_pairs={{0,16},{2,18},{4,20},{6,22},{8,24},{10,26},{12,28},{14,30},{16,0},... | collective-permute-start | bytes 184328 | tf_op jit(solution)/shard_map/ppermute | solution.py:880
  347.3 2.5 collective-permute-done.35.refs_1_
  349.8 2.4 collective-permute-start.37
  352.2 1.7 collective-permute-start.33
  354.0 2.0 collective-permute-done.37.refs_3_
  356.0 1.7 collective-permute-start.34
  357.7 1.7 fold.9.refs_4_
  359.4 0.9 collective-permute-start.38
  361.2 1.7 collective-permute-start.40
  362.9 4.3 %settle.1 = (bf16[32,72,384]{2,1,0:T(8,128)(2,1)}, bf16[32,72,384]{2,1,0:T(8,128)(2,1)}) custom-call(s32[2,32]{1,0:T(2,128)} %get-tuple-element.92.place, bf16[16,72,384]{2,1,0:T(8,128)(2,1)} %get-tuple-element.133.refs_0_, bf16[16,72,384]{2,1,0:T(8,128)(2,1)} %copy-done.8, bf16[16,72,384]{2,1,0:T(8,128)(2,1)} %get-tuple-element.135.refs_2_, ...), custom_call_target="tpu_custom_call" | custom-call | tf_op jit(solution)/shard_map/settle/pallas_call | solution.py:837
  367.3 2.1 collective-permute-done.39.refs_6_
  370.7 6.3 %unpack.1 = (f32[2,384,768]{2,1,0:T(8,128)}, f32[2,768,384]{2,1,0:T(8,128)}, f32[2,3,192,384]{3,2,1,0:T(8,128)}, f32[2,192,384]{2,1,0:T(8,128)}, f32[2,6,144,144...) custom-call(s32[1]{0:T(128)} %bitcast.2.digit_ref, ...), custom_call_target="tpu_custom_call" | custom-call | tf_op jit(solution)/shard_map/unpack/pallas_call | solution.py:1027
  377.0 1.0 fusion
  (134 shorter events, 16.8 us)
Async XLA Ops:
  7.2 360.0 %all-reduce.2.cloned.1.call-start = ((), (), s32[]{:S(2)}) async-start(), calls=%async_computation | async-start | bytes 4325376 | tf_op jit(solution)/shard_map/psum | solution.py:1126
  7.2 10.2 %collective-permute-start.1 = (bf16[2,3,192,384]{3,2,1,0:T(8,128)(2,1)}, bf16[2,3,192,384]{3,2,1,0:T(8,128)(2,1)S(1)}, u32[]{:S(2)}, u32[]{:S(2)}) collective-permute-start(bf16[2,3,192,384]{3,2,1,0:T(8,128)(2,1)} %bitcast.17), channel_id=1, source_target_pairs={{0,1},{1,0},{2,3},{3,2},{4,5},{5,4},{6,7},{7,6},{8,9},{9,8},{10,11... | collective-permute-start | bytes 2654216 | tf_op jit(solution)/shard_map/ppermute | solution.py:1041
  7.7 16.6 %collective-permute-start = (bf16[32,72,384]{2,1,0:T(8,128)(2,1)}, bf16[32,72,384]{2,1,0:T(8,128)(2,1)S(1)}, u32[]{:S(2)}, u32[]{:S(2)}) collective-permute-start(bf16[32,72,384]{2,1,0:T(8,128)(2,1)} %refs_2_.5), channel_id=1, source_target_pairs={{0,1},{1,0},{2,3},{3,2},{4,5},{5,4},{6,7},{7,6},{8,9},{9,8},{10,11... | collective-permute-start | bytes 5308424 | tf_op jit(solution)/shard_map/ppermute | solution.py:1041
  7.8 54.7 %collective-permute-start.9 = (bf16[32,72,384]{2,1,0:T(8,128)(2,1)}, bf16[32,72,384]{2,1,0:T(8,128)(2,1)}, u32[]{:S(2)}, u32[]{:S(2)}) collective-permute-start(bf16[32,72,384]{2,1,0:T(8,128)(2,1)} %refs_4_.5), channel_id=1, source_target_pairs={{0,1},{1,0},{2,3},{3,2},{4,5},{5,4},{6,7},{7,6},{8,9},{9,8},{10,11... | collective-permute-start | bytes 5308424 | tf_op jit(solution)/shard_map/ppermute | solution.py:1041
  8.3 9.0 %collective-permute-start.5 = (bf16[2,192,384]{2,1,0:T(8,128)(2,1)}, bf16[2,192,384]{2,1,0:T(8,128)(2,1)S(1)}, u32[]{:S(2)}, u32[]{:S(2)}) collective-permute-start(bf16[2,192,384]{2,1,0:T(8,128)(2,1)} %refs_8_.5), channel_id=1, source_target_pairs={{0,1},{1,0},{2,3},{3,2},{4,5},{5,4},{6,7},{7,6},{8,9},{9,8},{10,11... | collective-permute-start | bytes 884744 | tf_op jit(solution)/shard_map/ppermute | solution.py:1041
  8.3 7.2 %collective-permute-start.3 = (f32[2,2,192]{2,1,0:T(2,128)}, f32[2,2,192]{2,1,0:T(2,128)S(1)}, u32[]{:S(2)}, u32[]{:S(2)}) collective-permute-start(f32[2,2,192]{2,1,0:T(2,128)} %refs_11_.3), channel_id=1, source_target_pairs={{0,1},{1,0},{2,3},{3,2},{4,5},{5,4},{6,7},{7,6},{8,9},{9,8},{10,11... | collective-permute-start | bytes 9224 | tf_op jit(solution)/shard_map/ppermute | solution.py:1041
  15.5 1.4 collective-permute-start.4
  16.9 7.4 %collective-permute-start.6 = (bf16[2,384,768]{2,1,0:T(8,128)(2,1)}, bf16[2,384,768]{2,1,0:T(8,128)(2,1)}, u32[]{:S(2)}, u32[]{:S(2)}) collective-permute-start(bf16[2,384,768]{2,1,0:T(8,128)(2,1)} %refs_10_.3), channel_id=1, source_target_pairs={{0,1},{1,0},{2,3},{3,2},{4,5},{5,4},{6,7},{7,6},{8,9},{9,8},{10,11... | collective-permute-start | bytes 3538952 | tf_op jit(solution)/shard_map/ppermute | solution.py:1041
  17.3 7.1 %collective-permute-start.7 = (bf16[2,768,384]{2,1,0:T(8,128)(2,1)}, bf16[2,768,384]{2,1,0:T(8,128)(2,1)}, u32[]{:S(2)}, u32[]{:S(2)}) collective-permute-start(bf16[2,768,384]{2,1,0:T(8,128)(2,1)} %refs_12_.1), channel_id=1, source_target_pairs={{0,1},{1,0},{2,3},{3,2},{4,5},{5,4},{6,7},{7,6},{8,9},{9,8},{10,11... | collective-permute-start | bytes 3538952 | tf_op jit(solution)/shard_map/ppermute | solution.py:1041
  17.4 6.9 %collective-permute-start.2 = (f32[2,6,144,144]{3,2,1,0:T(8,128)}, f32[2,6,144,144]{3,2,1,0:T(8,128)}, u32[]{:S(2)}, u32[]{:S(2)}) collective-permute-start(f32[2,6,144,144]{3,2,1,0:T(8,128)} %refs_6_.4), channel_id=1, source_target_pairs={{0,1},{1,0},{2,3},{3,2},{4,5},{5,4},{6,7},{7,6},{8,9},{9,8},{10,11... | collective-permute-start | bytes 2985992 | tf_op jit(solution)/shard_map/ppermute | solution.py:1041
  62.1 1.5 collective-permute-start.8
  115.7 38.0 %collective-permute-start.10 = (bf16[1536,384]{1,0:T(8,128)(2,1)}, bf16[1536,384]{1,0:T(8,128)(2,1)S(1)}, u32[]{:S(2)}, u32[]{:S(2)}) collective-permute-start(bf16[1536,384]{1,0:T(8,128)(2,1)} %get-tuple-element.108), channel_id=1, source_target_pairs={{0,1},{1,0},{2,3},{3,2},{4,5},{5,4},{6,7},{7,6},{8,9},{9,8},{10,11... | collective-permute-start | bytes 3538952 | tf_op jit(solution)/shard_map/ppermute | solution.py:1041
  150.8 2.8 collective-permute-start.11
  151.1 8.0 %collective-permute-start.12 = (bf16[72,384]{1,0:T(8,128)(2,1)}, bf16[72,384]{1,0:T(8,128)(2,1)S(1)}, u32[]{:S(2)}, u32[]{:S(2)}) collective-permute-start(bf16[72,384]{1,0:T(8,128)(2,1)} %get-tuple-element.111), channel_id=1, source_target_pairs={{0,1},{1,0},{2,3},{3,2},{4,5},{5,4},{6,7},{7,6},{8,9},{9,8},{10,11... | collective-permute-start | bytes 165896 | tf_op jit(solution)/shard_map/ppermute | solution.py:1041
  184.6 3.1 collective-permute-start.13
  191.4 36.4 %copy-start.38 = (bf16[384,384]{1,0:T(8,128)(2,1)S(1)}, bf16[384,384]{1,0:T(8,128)(2,1)}, u32[]{:S(2)}) copy-start(bf16[384,384]{1,0:T(8,128)(2,1)} %get-tuple-element.140) | copy-start | bytes 884740
  191.4 80.9 %copy-start.37 = (bf16[384,384]{1,0:T(8,128)(2,1)S(1)}, bf16[384,384]{1,0:T(8,128)(2,1)}, u32[]{:S(2)}) copy-start(bf16[384,384]{1,0:T(8,128)(2,1)} %get-tuple-element.142) | copy-start | bytes 884740
  227.6 58.3 %collective-permute-start.19 = (bf16[1280,384]{1,0:T(8,128)(2,1)}, bf16[1280,384]{1,0:T(8,128)(2,1)S(1)}, u32[]{:S(2)}, u32[]{:S(2)}) collective-permute-start(bf16[1280,384]{1,0:T(8,128)(2,1)} %get-tuple-element.144), channel_id=1, source_target_pairs={{0,1},{1,0},{2,3},{3,2},{4,5},{5,4},{6,7},{7,6},{8,9},{9,8},{10,11... | collective-permute-start | bytes 2949128 | tf_op jit(solution)/shard_map/ppermute | solution.py:1041
  227.8 44.5 %collective-permute-start.16 = (bf16[384,384]{1,0:T(8,128)(2,1)S(1)}, bf16[384,384]{1,0:T(8,128)(2,1)S(1)}, u32[]{:S(2)}, u32[]{:S(2)}) collective-permute-start(bf16[384,384]{1,0:T(8,128)(2,1)S(1)} %copy-done.38), channel_id=1, source_target_pairs={{0,2},{2,0},{4,6},{6,4},{8,10},{10,8},{12,14},{14,12},{16,18},{18,... | collective-permute-start | bytes 884744 | tf_op jit(solution)/shard_map/ppermute | solution.py:880
  227.8 58.1 %collective-permute-start.17 = (bf16[384,384]{1,0:T(8,128)(2,1)}, bf16[384,384]{1,0:T(8,128)(2,1)S(1)}, u32[]{:S(2)}, u32[]{:S(2)}) collective-permute-start(bf16[384,384]{1,0:T(8,128)(2,1)} %get-tuple-element.141), channel_id=1, source_target_pairs={{0,4},{2,6},{4,0},{6,2},{8,12},{10,14},{12,8},{14,10},{16,20},{18,... | collective-permute-start | bytes 884744 | tf_op jit(solution)/shard_map/ppermute | solution.py:880
  272.3 13.6 %collective-permute-start.18 = (bf16[384,384]{1,0:T(8,128)(2,1)S(1)}, bf16[384,384]{1,0:T(8,128)(2,1)S(1)}, u32[]{:S(2)}, u32[]{:S(2)}) collective-permute-start(bf16[384,384]{1,0:T(8,128)(2,1)S(1)} %copy-done.37), channel_id=1, source_target_pairs={{0,6},{2,4},{4,2},{6,0},{8,14},{10,12},{12,10},{14,8},{16,22},{18,... | collective-permute-start | bytes 884744 | tf_op jit(solution)/shard_map/ppermute | solution.py:880
  272.3 87.1 %collective-permute-start.15 = (bf16[16,72,384]{2,1,0:T(8,128)(2,1)}, bf16[16,72,384]{2,1,0:T(8,128)(2,1)S(1)}, u32[]{:S(2)}, u32[]{:S(2)}) collective-permute-start(bf16[16,72,384]{2,1,0:T(8,128)(2,1)} %get-tuple-element.136), channel_id=1, source_target_pairs={{0,1},{1,0},{2,3},{3,2},{4,5},{5,4},{6,7},{7,6},{8,9},{9,8},{10,11... | collective-permute-start | bytes 2654216 | tf_op jit(solution)/shard_map/ppermute | solution.py:1041
  272.3 13.6 %copy-start.12 = (bf16[384,384]{1,0:T(8,128)(2,1)}, bf16[384,384]{1,0:T(8,128)(2,1)S(1)}, u32[]{:S(2)}) copy-start(bf16[384,384]{1,0:T(8,128)(2,1)S(1)} %collective-permute-done.16.refs_1_) | copy-start | bytes 884740
  272.3 88.0 %collective-permute-start.14 = (bf16[16,72,384]{2,1,0:T(8,128)(2,1)}, bf16[16,72,384]{2,1,0:T(8,128)(2,1)S(1)}, u32[]{:S(2)}, u32[]{:S(2)}) collective-permute-start(bf16[16,72,384]{2,1,0:T(8,128)(2,1)} %get-tuple-element.134), channel_id=1, source_target_pairs={{0,1},{1,0},{2,3},{3,2},{4,5},{5,4},{6,7},{7,6},{8,9},{9,8},{10,11... | collective-permute-start | bytes 2654216 | tf_op jit(solution)/shard_map/ppermute | solution.py:1041
  290.1 5.3 %collective-permute-start.20 = (bf16[96,384]{1,0:T(8,128)(2,1)}, bf16[96,384]{1,0:T(8,128)(2,1)S(1)}, u32[]{:S(2)}, u32[]{:S(2)}) collective-permute-start(bf16[96,384]{1,0:T(8,128)(2,1)} %get-tuple-element.146), channel_id=1, source_target_pairs={{0,8},{2,10},{4,12},{6,14},{8,0},{10,2},{12,4},{14,6},{16,24},{18,... | collective-permute-start | bytes 221192 | tf_op jit(solution)/shard_map/ppermute | solution.py:880
  291.9 8.9 %collective-permute-start.21 = (bf16[96,384]{1,0:T(8,128)(2,1)}, bf16[96,384]{1,0:T(8,128)(2,1)S(1)}, u32[]{:S(2)}, u32[]{:S(2)}) collective-permute-start(bf16[96,384]{1,0:T(8,128)(2,1)} %get-tuple-element.147), channel_id=1, source_target_pairs={{0,16},{2,18},{4,20},{6,22},{8,24},{10,26},{12,28},{14,30},{16,0},... | collective-permute-start | bytes 221192 | tf_op jit(solution)/shard_map/ppermute | solution.py:880
  294.3 7.4 %collective-permute-start.22 = (bf16[96,384]{1,0:T(8,128)(2,1)}, bf16[96,384]{1,0:T(8,128)(2,1)S(1)}, u32[]{:S(2)}, u32[]{:S(2)}) collective-permute-start(bf16[96,384]{1,0:T(8,128)(2,1)} %get-tuple-element.148), channel_id=1, source_target_pairs={{0,24},{2,26},{4,28},{6,30},{8,16},{10,18},{12,20},{14,22},{16,8},... | collective-permute-start | bytes 221192 | tf_op jit(solution)/shard_map/ppermute | solution.py:880
  295.4 18.8 %copy-start.22 = (bf16[96,384]{1,0:T(8,128)(2,1)}, bf16[96,384]{1,0:T(8,128)(2,1)S(1)}, u32[]{:S(2)}) copy-start(bf16[96,384]{1,0:T(8,128)(2,1)S(1)} %collective-permute-done.20.refs_1_) | copy-start | bytes 221188
  295.4 7.6 %collective-permute-start.23 = (bf16[320,384]{1,0:T(8,128)(2,1)}, bf16[320,384]{1,0:T(8,128)(2,1)S(1)}, u32[]{:S(2)}, u32[]{:S(2)}) collective-permute-start(bf16[320,384]{1,0:T(8,128)(2,1)} %get-tuple-element.150), channel_id=1, source_target_pairs={{0,2},{2,0},{4,6},{6,4},{8,10},{10,8},{12,14},{14,12},{16,18},{18,... | collective-permute-start | bytes 737288 | tf_op jit(solution)/shard_map/ppermute | solution.py:880
  300.8 13.3 %copy-start.23 = (bf16[96,384]{1,0:T(8,128)(2,1)}, bf16[96,384]{1,0:T(8,128)(2,1)S(1)}, u32[]{:S(2)}) copy-start(bf16[96,384]{1,0:T(8,128)(2,1)S(1)} %collective-permute-done.21.refs_2_) | copy-start | bytes 221188
  300.8 13.3 %collective-permute-start.24 = (bf16[320,384]{1,0:T(8,128)(2,1)}, bf16[320,384]{1,0:T(8,128)(2,1)S(1)}, u32[]{:S(2)}, u32[]{:S(2)}) collective-permute-start(bf16[320,384]{1,0:T(8,128)(2,1)} %get-tuple-element.151), channel_id=1, source_target_pairs={{0,4},{2,6},{4,0},{6,2},{8,12},{10,14},{12,8},{14,10},{16,20},{18,... | collective-permute-start | bytes 737288 | tf_op jit(solution)/shard_map/ppermute | solution.py:880
  301.7 12.5 %collective-permute-start.25 = (bf16[320,384]{1,0:T(8,128)(2,1)}, bf16[320,384]{1,0:T(8,128)(2,1)S(1)}, u32[]{:S(2)}, u32[]{:S(2)}) collective-permute-start(bf16[320,384]{1,0:T(8,128)(2,1)} %get-tuple-element.152), channel_id=1, source_target_pairs={{0,6},{2,4},{4,2},{6,0},{8,14},{10,12},{12,10},{14,8},{16,22},{18,... | collective-permute-start | bytes 737288 | tf_op jit(solution)/shard_map/ppermute | solution.py:880
  317.0 4.4 %collective-permute-start.29 = (bf16[80,384]{1,0:T(8,128)(2,1)}, bf16[80,384]{1,0:T(8,128)(2,1)S(1)}, u32[]{:S(2)}, u32[]{:S(2)}) collective-permute-start(bf16[80,384]{1,0:T(8,128)(2,1)} %get-tuple-element.155), channel_id=1, source_target_pairs={{0,8},{2,10},{4,12},{6,14},{8,0},{10,2},{12,4},{14,6},{16,24},{18,... | collective-permute-start | bytes 184328 | tf_op jit(solution)/shard_map/ppermute | solution.py:880
  317.1 5.4 %collective-permute-start.30 = (bf16[80,384]{1,0:T(8,128)(2,1)}, bf16[80,384]{1,0:T(8,128)(2,1)S(1)}, u32[]{:S(2)}, u32[]{:S(2)}) collective-permute-start(bf16[80,384]{1,0:T(8,128)(2,1)} %get-tuple-element.156), channel_id=1, source_target_pairs={{0,16},{2,18},{4,20},{6,22},{8,24},{10,26},{12,28},{14,30},{16,0},... | collective-permute-start | bytes 184328 | tf_op jit(solution)/shard_map/ppermute | solution.py:880
  319.9 6.4 %collective-permute-start.31 = (bf16[80,384]{1,0:T(8,128)(2,1)}, bf16[80,384]{1,0:T(8,128)(2,1)S(1)}, u32[]{:S(2)}, u32[]{:S(2)}) collective-permute-start(bf16[80,384]{1,0:T(8,128)(2,1)} %get-tuple-element.157), channel_id=1, source_target_pairs={{0,24},{2,26},{4,28},{6,30},{8,16},{10,18},{12,20},{14,22},{16,8},... | collective-permute-start | bytes 184328 | tf_op jit(solution)/shard_map/ppermute | solution.py:880
  321.5 12.7 %copy-start.28 = (bf16[80,384]{1,0:T(8,128)(2,1)}, bf16[80,384]{1,0:T(8,128)(2,1)S(1)}, u32[]{:S(2)}) copy-start(bf16[80,384]{1,0:T(8,128)(2,1)S(1)} %collective-permute-done.29.refs_5_) | copy-start | bytes 184324
  321.5 6.7 %collective-permute-start.26 = (bf16[96,384]{1,0:T(8,128)(2,1)}, bf16[96,384]{1,0:T(8,128)(2,1)S(1)}, u32[]{:S(2)}, u32[]{:S(2)}) collective-permute-start(bf16[96,384]{1,0:T(8,128)(2,1)} %get-tuple-element.153.refs_0_), channel_id=1, source_target_pairs={{0,8},{2,10},{4,12},{6,14},{8,0},{10,2},{12,4},{14,6},{16,24},{18,... | collective-permute-start | bytes 221192 | tf_op jit(solution)/shard_map/ppermute | solution.py:880
  322.4 5.8 %collective-permute-start.27 = (bf16[96,384]{1,0:T(8,128)(2,1)}, bf16[96,384]{1,0:T(8,128)(2,1)S(1)}, u32[]{:S(2)}, u32[]{:S(2)}) collective-permute-start(bf16[96,384]{1,0:T(8,128)(2,1)} %get-tuple-element.153.refs_0_), channel_id=1, source_target_pairs={{0,16},{2,18},{4,20},{6,22},{8,24},{10,26},{12,28},{14,30},{16,0},... | collective-permute-start | bytes 221192 | tf_op jit(solution)/shard_map/ppermute | solution.py:880
  326.3 7.9 %collective-permute-start.28 = (bf16[96,384]{1,0:T(8,128)(2,1)}, bf16[96,384]{1,0:T(8,128)(2,1)S(1)}, u32[]{:S(2)}, u32[]{:S(2)}) collective-permute-start(bf16[96,384]{1,0:T(8,128)(2,1)} %get-tuple-element.153.refs_0_), channel_id=1, source_target_pairs={{0,24},{2,26},{4,28},{6,30},{8,16},{10,18},{12,20},{14,22},{16,8},... | collective-permute-start | bytes 221192 | tf_op jit(solution)/shard_map/ppermute | solution.py:880
  336.6 24.5 %collective-permute-start.32 = (bf16[384,384]{1,0:T(8,128)(2,1)}, bf16[384,384]{1,0:T(8,128)(2,1)S(1)}, u32[]{:S(2)}, u32[]{:S(2)}) collective-permute-start(bf16[384,384]{1,0:T(8,128)(2,1)} %get-tuple-element.158.refs_0_), channel_id=1, source_target_pairs={{0,2},{2,0},{4,6},{6,4},{8,10},{10,8},{12,14},{14,12},{16,18},{18,... | collective-permute-start | bytes 884744 | tf_op jit(solution)/shard_map/ppermute | solution.py:880
  336.7 13.1 %collective-permute-start.35 = (bf16[80,384]{1,0:T(8,128)(2,1)}, bf16[80,384]{1,0:T(8,128)(2,1)S(1)}, u32[]{:S(2)}, u32[]{:S(2)}) collective-permute-start(bf16[80,384]{1,0:T(8,128)(2,1)} %get-tuple-element.159.refs_0_), channel_id=1, source_target_pairs={{0,8},{2,10},{4,12},{6,14},{8,0},{10,2},{12,4},{14,6},{16,24},{18,... | collective-permute-start | bytes 184328 | tf_op jit(solution)/shard_map/ppermute | solution.py:880
  342.8 9.4 %collective-permute-start.36 = (bf16[80,384]{1,0:T(8,128)(2,1)}, bf16[80,384]{1,0:T(8,128)(2,1)S(1)}, u32[]{:S(2)}, u32[]{:S(2)}) collective-permute-start(bf16[80,384]{1,0:T(8,128)(2,1)} %get-tuple-element.159.refs_0_), channel_id=1, source_target_pairs={{0,16},{2,18},{4,20},{6,22},{8,24},{10,26},{12,28},{14,30},{16,0},... | collective-permute-start | bytes 184328 | tf_op jit(solution)/shard_map/ppermute | solution.py:880
  349.8 6.2 %collective-permute-start.37 = (bf16[80,384]{1,0:T(8,128)(2,1)}, bf16[80,384]{1,0:T(8,128)(2,1)S(1)}, u32[]{:S(2)}, u32[]{:S(2)}) collective-permute-start(bf16[80,384]{1,0:T(8,128)(2,1)} %get-tuple-element.159.refs_0_), channel_id=1, source_target_pairs={{0,24},{2,26},{4,28},{6,30},{8,16},{10,18},{12,20},{14,22},{16,8},... | collective-permute-start | bytes 184328 | tf_op jit(solution)/shard_map/ppermute | solution.py:880
  352.2 15.0 %collective-permute-start.33 = (bf16[384,384]{1,0:T(8,128)(2,1)}, bf16[384,384]{1,0:T(8,128)(2,1)S(1)}, u32[]{:S(2)}, u32[]{:S(2)}) collective-permute-start(bf16[384,384]{1,0:T(8,128)(2,1)} %get-tuple-element.158.refs_0_), channel_id=1, source_target_pairs={{0,4},{2,6},{4,0},{6,2},{8,12},{10,14},{12,8},{14,10},{16,20},{18,... | collective-permute-start | bytes 884744 | tf_op jit(solution)/shard_map/ppermute | solution.py:880
  356.0 11.3 %collective-permute-start.34 = (bf16[384,384]{1,0:T(8,128)(2,1)}, bf16[384,384]{1,0:T(8,128)(2,1)S(1)}, u32[]{:S(2)}, u32[]{:S(2)}) collective-permute-start(bf16[384,384]{1,0:T(8,128)(2,1)} %get-tuple-element.158.refs_0_), channel_id=1, source_target_pairs={{0,6},{2,4},{4,2},{6,0},{8,14},{10,12},{12,10},{14,8},{16,22},{18,... | collective-permute-start | bytes 884744 | tf_op jit(solution)/shard_map/ppermute | solution.py:880
  359.4 7.9 %collective-permute-start.38 = (bf16[320,384]{1,0:T(8,128)(2,1)}, bf16[320,384]{1,0:T(8,128)(2,1)S(1)}, u32[]{:S(2)}, u32[]{:S(2)}) collective-permute-start(bf16[320,384]{1,0:T(8,128)(2,1)} %fold.9.refs_4_), channel_id=1, source_target_pairs={{0,2},{2,0},{4,6},{6,4},{8,10},{10,8},{12,14},{14,12},{16,18},{18,... | collective-permute-start | bytes 737288 | tf_op jit(solution)/shard_map/ppermute | solution.py:880
  360.3 9.0 %collective-permute-start.39 = (bf16[320,384]{1,0:T(8,128)(2,1)}, bf16[320,384]{1,0:T(8,128)(2,1)S(1)}, u32[]{:S(2)}, u32[]{:S(2)}) collective-permute-start(bf16[320,384]{1,0:T(8,128)(2,1)} %fold.9.refs_4_), channel_id=1, source_target_pairs={{0,4},{2,6},{4,0},{6,2},{8,12},{10,14},{12,8},{14,10},{16,20},{18,... | collective-permute-start | bytes 737288 | tf_op jit(solution)/shard_map/ppermute | solution.py:880
  361.2 8.2 %collective-permute-start.40 = (bf16[320,384]{1,0:T(8,128)(2,1)}, bf16[320,384]{1,0:T(8,128)(2,1)S(1)}, u32[]{:S(2)}, u32[]{:S(2)}) collective-permute-start(bf16[320,384]{1,0:T(8,128)(2,1)} %fold.9.refs_4_), channel_id=1, source_target_pairs={{0,6},{2,4},{4,2},{6,0},{8,14},{10,12},{12,10},{14,8},{16,22},{18,... | collective-permute-start | bytes 737288 | tf_op jit(solution)/shard_map/ppermute | solution.py:880
  (33 other events, 131.0 us)
Sparse Core Ops, SparseCore 0:
  185.0 167.7 all-reduce.1
where the time goes:
time: 394 us; the launch traced here: 387 us
  Pallas kernels  214 us (54%)
  starting transfers between devices  88.1 us (22%)
  waiting for transfers between devices  58.2 us (15%)
  between operations  14.6 us (4%)
  local copies, waits for them, and re-layouts  11.4 us (3%)
    pallas_call x5, Pallas kernels, run_block(): pl.pallas_call(functools.partial(block_kernel, [*ins, *outs, *scratch], s...  184 us
    ppermute x24, starting transfers between devices, with_peer(): lax.ppermute(value, DP, [(d, d ^ k * stride) for d in range(devices)])  82.9 us
    ppermute x24, waiting for transfers between devices, with_peer(): lax.ppermute(value, DP, [(d, d ^ k * stride) for d in range(devices)])  42.3 us
    ppermute x17, waiting for transfers between devices, across(): return lax.ppermute(value, TENSOR, [(0, 1), (1, 0)])  15.8 us
    pallas_call x5, Pallas kernels, advance(): pl.pallas_call(functools.partial(local_kernel, jobs), out_shape=tuple((ja...  11.4 us
    unnamed x81, local copies, waits for them, and re-layouts  10.4 us
  transfers between devices with their start and end apart: 42, of which 17 were waited for; matrix products, arithmetic and copies ran while one was open for 0% of the time, Pallas kernels for 34%

commit v1 on v0

--- a/solution.py
+++ b/solution.py
@@ -154,6 +154,7 @@
         in_specs=[smem, smem, smem],
         out_specs=(smem, smem, smem),
         scratch_shapes=[pltpu.SMEM((home,), I32) for _ in range(6)],
+        cost_estimate=pl.CostEstimate(flops=5 * 10**9, bytes_accessed=2**24, transcendentals=0),
         name="plan",
     )(part, token_mask, shift_next)
 
@@ -214,6 +215,9 @@
     spare_lane = [lane == spot for spot in spots]
     spare_two = [(lane == spot) | (lane == spot + 1) for spot in spots]
     one = jnp.ones((), BF16)
+    pitch = -(-win // 256) * 256
+    blank_lanes = jnp.zeros((win, pitch - win), BF16)
+    blank_rows = jnp.zeros((pitch - win, 128), BF16)
     wide_step = TILE * win
 
     def row(table):
@@ -313,9 +317,9 @@
                 ref.bias[k] = ref.bias[k] * (1.0 / LN2)
         sums = [ref.acc_small] if mixer or attention else []
         if mixer:
-            sums += [ref.acc_up, ref.acc_down, ref.acc_hidden]
+            sums += [ref.acc_up, ref.acc_down, ref.acc_out, ref.acc_hidden]
         if attention:
-            sums += [ref.acc_in, ref.acc_out, ref.acc_earth, ref.acc_entry]
+            sums += [ref.acc_in, ref.acc_earth, ref.acc_entry]
         for table in sums:
             table[...] = jnp.zeros_like(table)
 
@@ -369,7 +373,7 @@
         for g in range(groups):
             span = [slice(j * width + g * 128, j * width + (g + 1) * 128) for j in range(3)]
             q, k, v = (ref.qkv[rows, cols] for cols in span)
-            total = None
+            total = []
             for u in range(per_group):
                 head = g * per_group + u
                 spare = spare_lane[u]
@@ -377,9 +381,11 @@
                 s = s + ref.bias[head]
                 low = jnp.exp2(s - jnp.max(s, axis=-1, keepdims=True)).astype(BF16)
                 ref.probs[w, head] = low
-                keep = jnp.broadcast_to(head_keep[u], (win, 128))
-                got = mm(low, jnp.concatenate([v * keep, keep], axis=1))
-                total = got if total is None else total + got
+                total.append(jnp.concatenate([low, blank_lanes], axis=1))
+            tall = [value for keep in head_keep for value in (v * keep, blank_rows)]
+            ones = [value for keep in head_keep for value in (jnp.broadcast_to(keep, (win, 128)), blank_rows)]
+            tall = jnp.concatenate([jnp.concatenate(tall, axis=0), jnp.concatenate(ones, axis=0)], axis=1)
+            total = mm(jnp.concatenate(total, axis=1), tall)
             inverse = 1.0 / total[:, 128:]
             cols = slice(g * 128, (g + 1) * 128)
             ref.att[rows, cols] = (total[:, :128] * inverse).astype(BF16)
@@ -410,7 +416,6 @@
             r = jnp.concatenate(parts, axis=0)
             r_low = r.astype(BF16)
             ref.rr[rows, :] = r_low
-        d_h2 = None
         for s, off in pieces:
             cols = slice(off, off + 384)
             at = off + s * hidden_part
@@ -420,7 +425,6 @@
                 g, slope = gelu_pair(u)
                 g = g.astype(BF16)
                 ref.act[rows, span] = g
-                result = result + mm(g, down_sides[s][cols, :])
                 if not mixer:
                     ref.slope[rows, span] = slope.astype(BF16)
             else:
@@ -430,8 +434,12 @@
                 ref.acc_hidden[:, span] += fold_rows(du)
                 du = du.astype(BF16)
                 ref.du[rows, span] = du
-                d = mm_nt(du, up_sides[s][:, cols])
-                d_h2 = d if d_h2 is None else d_h2 + d
+        sides = [slice(s * hidden_part, (s + 1) * hidden_part) for s in range(2)]
+        if ahead:
+            for side, cols in zip(down_sides, sides):
+                result = result + mm(ref.act[rows, cols], side[...])
+        if mixer:
+            d_h2 = mm_nt(ref.du[rows, sides[0]], up_sides[0][...]) + mm_nt(ref.du[rows, sides[1]], up_sides[1][...])
         if ahead:
             for j in range(TILE):
                 i = w0 + tile * TILE + j
@@ -477,6 +485,7 @@
             cols = slice(at, at + 256)
             ref.acc_down[:, cols] += mm(r_turned, ref.act[:, cols])
             ref.acc_up[:, cols] += mm(h_turned, ref.du[:, cols])
+        ref.acc_out[...] += mm(ref.att[...].T, ref.da[...])
         return c
 
     def attend_back(pair, c):
@@ -503,12 +512,13 @@
                     ds = ds.astype(BF16)
                     dk.append(mm(q_turned[cut], ds))
                     dv.append(mm(do_turned[cut], low))
-                    got = mm(ds, k * head_keep[u])
-                    dq[:] = [got if not dq else dq[0] + got]
+                    dq.append(jnp.concatenate([ds, blank_lanes], axis=1))
                 ref.acc_earth[head] += total
             for j, rows in enumerate(spans):
                 dq, dk, dv = loaded[j][6:]
-                dq = dq[0] * scale
+                k = loaded[j][1]
+                tall = [value for keep in head_keep for value in (k * keep, blank_rows)]
+                dq = mm(jnp.concatenate(dq, axis=1), jnp.concatenate(tall, axis=0)) * scale
                 dk = (jnp.concatenate(dk, axis=0) * LN2).T
                 dv = jnp.concatenate(dv, axis=0).T
                 for at, value in ((0, dq), (2, dv)):
@@ -536,7 +546,6 @@
         return c
 
     def weight_grads(_, c):
-        ref.acc_out[...] += mm(ref.att[...].T, ref.da[...])
         turned = ref.h1[...].T
         for j in range(3):
             cols = slice(j * width, (j + 1) * width)
@@ -578,8 +587,10 @@
                     cols = slice(base + at, base + at + width)
                     pack[at : at + width, :] = ref.acc_up[:, cols].astype(BF16)
                     pack[hidden_part + at : hidden_part + at + width, :] = ref.acc_down[:, cols].astype(BF16)
-                if pack.shape[0] > 2 * hidden_part:
-                    pack[2 * hidden_part :, :] = jnp.zeros_like(pack[2 * hidden_part :, :])
+                low, high = 2 * hidden_part, 2 * hidden_part + part
+                pack[low:high, :] = ref.acc_out[s * part : (s + 1) * part, :].astype(BF16)
+                if pack.shape[0] > high:
+                    pack[high:, :] = jnp.zeros_like(pack[high:, :])
             ref.sums_small[...] = jnp.sum(ref.acc_small[...], axis=1)
             ref.sums_hidden[...] = jnp.sum(ref.acc_hidden[...], axis=0, keepdims=True)
         if attention:
@@ -597,7 +608,6 @@
                 for j, cut in enumerate(cuts):
                     at = layout.inward + j * part
                     pack[at : at + part, :] = ref.acc_in[:, cut].T.astype(BF16)
-                pack[layout.out : layout.out + part, :] = ref.acc_out[s * part : (s + 1) * part, :].astype(BF16)
                 earth = [ref.acc_earth[s * own_heads + k] for k in range(own_heads)]
                 for k, value in enumerate(earth):
                     row_at = layout.earth + (k // 3) * win
@@ -622,7 +632,7 @@
 
 def pack_rows(width, own_heads, win):
     counts = dict(
-        inward=3 * width // 2, out=width // 2, earth=own_heads // 3 * win, rest=win // 3, small=16, total=0
+        inward=3 * width // 2, earth=own_heads // 3 * win, rest=win // 3, small=16, total=0
     )
     layout, at = {}, 0
     for name, count in counts.items():
@@ -718,7 +728,7 @@
         take_block(in_own=g.in_own, in_oth=g.in_oth)
     if attention:
         take(None, sums_small=g.sums_small, sums_hidden=g.sums_hidden)
-        carry_in(qkv=g.qkv, probs=g.probs, att=g.att, h1=g.h1, da=g.da, do=g.do, aug=g.aug)
+        carry_in(qkv=g.qkv, probs=g.probs, h1=g.h1, da=g.da, do=g.do, aug=g.aug)
     elif not ahead:
         carry_in(att=g.att, inverse=g.inverse, h2=g.h2, act=g.act, slope=g.slope)
 
@@ -734,7 +744,7 @@
     if (ahead and shifted) or (attention and not shifted):
         give(keep=(cap // parts,) + half_shape, send=(cap // parts,) + half_shape)
     if mixer:
-        pack = (padded(2 * hidden_part, devices), width)
+        pack = (padded(2 * hidden_part + width // 2, devices), width)
         give(pack_own=pack, pack_oth=pack)
         give(F32, sums_small=(6, width), sums_hidden=(1, hidden))
     if attention:
@@ -761,11 +771,11 @@
     if mixer:
         hold(rs=halves, rr=flat(1), du=(rows, hidden), spread=(width, width))
         scratch.update(r_sem=pltpu.SemaphoreType.DMA((cap, 2)))
-        hold(F32, acc_up=(width, hidden), acc_down=(width, hidden), acc_hidden=(8, hidden))
+        hold(F32, acc_up=(width, hidden), acc_down=(width, hidden), acc_hidden=(8, hidden), acc_out=(width, width))
     if attention:
         hold(dqkv=flat(3))
-        hold(F32, acc_in=(width, 3 * width), acc_out=(width, width))
-        hold(F32, acc_earth=(heads, win, win), acc_entry=(8, 3 * width))
+        hold(F32, acc_in=(width, 3 * width), acc_earth=(heads, win, win))
+        hold(F32, acc_entry=(8, 3 * width))
     if mixer or attention:
         hold(F32, acc_small=(6, 8, width))
 
@@ -969,7 +979,8 @@
     refs = list(refs)
     pieces = [[refs.pop(0) for _ in range(count)] for _ in range(2)]
     whole_two = refs.pop(0)
-    up, down, inward, out, earth, small, hidden, entry, *joined = refs
+    up, down, inward, out, earth, hidden, entry, *rest_refs = refs
+    small, joined = rest_refs[:6], rest_refs[6:]
     digit = digit_ref[0]
     for parts, whole in zip(pieces, joined):
         rows = parts[0].shape[0]
@@ -995,7 +1006,8 @@
 
         for j in range(3):
             inward[b, j] = lines_of(layout.inward, j * part, part)
-        out[b] = lines_of(layout.out, 0, part)
+        low = base + 2 * hidden_part
+        out[b] = pack[low : low + part, :].astype(F32)
         rest = lines_of(layout.rest, 0, third)
         rest = jnp.concatenate([rest[:, k * 128 : (k + 1) * 128] for k in range(3)], axis=0)
         for k in range(earth.shape[1]):
@@ -1003,7 +1015,8 @@
             earth[b, k, :, :128] = main[:, (k % 3) * 128 : (k % 3 + 1) * 128]
             earth[b, k, :, 128:] = rest[:, k * (win - 128) : (k + 1) * (win - 128)]
         lines = lines_of(layout.small, 0, 16)
-        small[b] = lines[:6]
+        for k, table in enumerate(small):
+            table[b : b + 1, :] = lines[k : k + 1]
         for j, at in enumerate(range(0, hidden_part, width)):
             hidden[b : b + 1, at : at + width] = lines[6 + j : 7 + j]
         last = lines[6 + hidden_part // width : 7 + hidden_part // width]
@@ -1019,10 +1032,9 @@
         (2, 3, width // 2, width),
         (2, width // 2, width),
         (2, own_heads, win, win),
-        (2, 6, width),
         (2, hidden_part),
         (2, 2, width // 2),
-    )
+    ) + ((2, width),) * 6
     count = len(hidden_parts)
     return pl.pallas_call(
         functools.partial(unpack_kernel, pack_rows(width, own_heads, win), count),
@@ -1133,7 +1145,9 @@
         if which:
             (do,) = advance([sum_mixer_one], digits, do)
         halves.append(run((False, False, True), 0, ahead_one, mixer_one, Bag(do=do), first, split=(which, PARTS)))
-        across_one.append(across(halves[-1].pack_oth))
+        far, parts = lax.optimization_barrier((halves[-1].pack_oth, sum_mixer_one.parts))
+        sum_mixer_one.parts = parts
+        across_one.append(across(far))
     sum_attention_one = DpSum([half_of.pack_own for half_of in halves] + across_one)
     recv_a = [across(half_of.send) for half_of in halves]
     sums = [sum_mixer_one, sum_attention_one]
@@ -1142,25 +1156,25 @@
     tokens_grad, block_output = settle(
         place, [half_of.keep for half_of in halves] + recv_a, [mixer_two.keep, recv_b]
     )
-    g_up, g_down, g_in, g_out, g_earth, small, hidden, entry = unpack(
+    g_up, g_down, g_in, g_out, g_earth, hidden, entry, *small = unpack(
         digits[:1], sum_mixer_one.parts, sum_attention_one.parts, sum_two, width, hidden_part, own_heads, win
     )
     return (
         block_output,
         tokens_grad,
-        small[:, 0],
-        small[:, 1],
+        small[0],
+        small[1],
         jnp.transpose(g_in, (0, 3, 1, 2)),
         entry,
         g_earth,
         g_out,
-        small[:, 2],
-        small[:, 3],
-        small[:, 4],
+        small[2],
+        small[3],
+        small[4],
         g_up,
         hidden,
         g_down,
-        small[:, 5],
+        small[5],
     )
 
 

time: 394 us -> 370 us (0.939)
  Pallas kernels: 214 us -> 101 us
  starting transfers between devices: 88.1 us -> 155 us
  waiting for transfers between devices: 58.2 us -> 82.8 us
    pallas_call x5, Pallas kernels: 184 us -> 71.4 us  [run_block(): pl.pallas_call(functools.partial(block_kernel, [*ins, *outs, *scratch], s...]
    ppermute x24, starting transfers between devices: 82.9 us -> 150 us  [with_peer(): lax.ppermute(value, DP, [(d, d ^ k * stride) for d in range(devices)])]
    psum x1, waiting for transfers between devices: 0.02 us -> 29.1 us  [local(): sum_two = lax.psum(pack_two, DP)]
    ppermute x24, waiting for transfers between devices: 42.3 us -> 35.3 us  [with_peer(): lax.ppermute(value, DP, [(d, d ^ k * stride) for d in range(devices)])]
    unnamed x81 -> x74, local copies, waits for them, and re-layouts: 10.4 us -> 9.4 us
  transfers between devices with their start and end apart: 42 -> 42, of which waited for: 17 -> 20; matrix products, arithmetic and copies ran while one was open for 0% -> 0% of each run, Pallas kernels for 34% -> 18%
where the time goes in v1:
time: 370 us; the launch traced here: 364 us
  starting transfers between devices  155 us (42%)
  Pallas kernels  101 us (27%)
  waiting for transfers between devices  82.8 us (22%)
  between operations  14.8 us (4%)
  local copies, waits for them, and re-layouts  9.4 us (3%)
    ppermute x24, starting transfers between devices, with_peer(): lax.ppermute(value, DP, [(d, d ^ k * stride) for d in range(devices)])  150 us
    pallas_call x5, Pallas kernels, run_block(): pl.pallas_call(functools.partial(block_kernel, [*ins, *outs, *scratch], s...  71.4 us
    ppermute x24, waiting for transfers between devices, with_peer(): lax.ppermute(value, DP, [(d, d ^ k * stride) for d in range(devices)])  35.3 us
    psum x1, waiting for transfers between devices, local(): sum_two = lax.psum(pack_two, DP)  29.1 us
    ppermute x17, waiting for transfers between devices, across(): return lax.ppermute(value, TENSOR, [(0, 1), (1, 0)])  18.3 us
    pallas_call x5, Pallas kernels, advance(): pl.pallas_call(functools.partial(local_kernel, jobs), out_shape=tuple((ja...  11.5 us
    unnamed x74, local copies, waits for them, and re-layouts  9.4 us
  transfers between devices with their start and end apart: 42, of which 20 were waited for; matrix products, arithmetic and copies ran while one was open for 0% of the time, Pallas kernels for 18%

profile of v1, /device:TPU:0, one launch (start us, length us, event | category | flops | bytes accessed | tf_op | source)
XLA Modules:
  0.0 363.6 jit_solution(810295884301871592)
XLA Ops:
  8.8 6.7 %collective-permute-done.3.refs_10_.refs_12_ = f32[2,2,192]{2,1,0:T(2,128)S(1)} collective-permute-done((f32[2,2,192]{2,1,0:T(2,128)}, f32[2,2,192]{2,1,0:T(2,128)S(1)}, u32[]{:S(2)}, u32[]{:S(2)}) %collective-permute-start.3) | collective-permute-done | bytes 3104 | tf_op jit(solution)/shard_map/ppermute | solution.py:1053
  15.9 1.0 collective-permute-done.4.refs_12_.refs_14_
  17.8 3.6 plan.1
  21.4 2.9 collective-permute-done.2.refs_5_.refs_7_
  24.3 1.2 copy-done
  25.5 17.7 %ahead1.1 = (bf16[2304,1152]{1,0:T(8,128)(2,1)}, bf16[16,12,144,144]{3,2,1,0:T(8,128)(2,1)}, bf16[2304,384]{1,0:T(8,128)(2,1)}, bf16[2304,384]{1,0:T(8,128)(2,1)...) custom-call(s32[8]{0:T(128)} %get-tuple-element.102.refs_0_, ...), custom_call_target="tpu_custom_call" | custom-call | flops 127401984 | bytes 221184 | tf_op jit(solution)/shard_map/ahead1/pallas_call | solution.py:783
  43.7 1.1 collective-permute-done.8.refs_3_
  45.4 15.5 %aheadmixer2.1 = (bf16[2304,1152]{1,0:T(8,128)(2,1)}, bf16[16,12,144,144]{3,2,1,0:T(8,128)(2,1)}, bf16[2304,384]{1,0:T(8,128)(2,1)}, bf16[2304,384]{1,0:T(8,128)...) custom-call(s32[8]{0:T(128)} %get-tuple-element.102.refs_0_, ...), custom_call_target="tpu_custom_call" | custom-call | flops 254803968 | bytes 442368 | tf_op jit(solution)/shard_map/aheadmixer2/pallas_call | solution.py:783
  61.3 12.6 %attention2.1 = (bf16[16,2,72,384]{3,2,1,0:T(8,128)(2,1)}, bf16[72,384]{1,0:T(8,128)(2,1)}, bf16[1024,384]{1,0:T(8,128)(2,1)}, bf16[1024,384]{1,0:T(8,128)(2,1)}) custom-call(s32[8]{0:T(128)} %get-tuple-element.102.refs_0_, s32[8,16]{1,0:T(8,128)} %get-tuple-element.103.refs_1_, bf16[16,2,72,384]{3,2,1,0:T(8,128)(2,1)} %get-tuple-element.104.refs_2_, ...), custom_call_target="tpu_custom_call" | custom-call | flops 127401984 | bytes 221184 | tf_op jit(solution)/shard_map/attention2/pallas_call | solution.py:783
  74.5 2.0 collective-permute-done.11.refs_3_
  77.8 4.1 %stack.13 = bf16[2816,384]{1,0:T(8,128)(2,1)} custom-call(bf16[1792,384]{1,0:T(8,128)(2,1)} %get-tuple-element.115.refs_0_, bf16[1792,384]{1,0:T(8,128)(2,1)} %copy-done.4, bf16[1024,384]{1,0:T(8,128)(2,1)} %get-tuple-element.117.refs_2_, bf16[1024,384]{1,0:T(8,128)(2,1)} %copy-done.7), custom_call_target="tpu_custom_call" | custom-call | tf_op jit(solution)/shard_map/stack/pallas_call | solution.py:905
  82.5 13.2 %mixer1.1 = (bf16[2304,384]{1,0:T(8,128)(2,1)}, bf16[2304,384]{1,0:T(8,128)(2,1)}, bf16[2304,384]{1,0:T(8,128)(2,1)}, bf16[1792,384]{1,0:T(8,128)(2,1)}, bf16[17...) custom-call(s32[8]{0:T(128)} %get-tuple-element.102.refs_0_, s32[8,16]{1,0:T(8,128)} %get-tuple-element.103.refs_1_, ...), custom_call_target="tpu_custom_call" | custom-call | flops 127401984 | bytes 221184 | tf_op jit(solution)/shard_map/mixer1/pallas_call | solution.py:783
  96.5 2.5 collective-permute-done.13.refs_1_
  99.1 1.1 copy-done.3
  100.1 3.0 fold.5
  103.1 35.0 %collective-permute-start.16 = (bf16[448,384]{1,0:T(8,128)(2,1)}, bf16[448,384]{1,0:T(8,128)(2,1)S(1)}, u32[]{:S(2)}, u32[]{:S(2)}) collective-permute-start(bf16[448,384]{1,0:T(8,128)(2,1)} %get-tuple-element.149), channel_id=1, source_target_pairs={{0,2},{2,0},{4,6},{6,4},{8,10},{10,8},{12,14},{14,12},{16,18},{18,... | collective-permute-start | bytes 1032200 | tf_op jit(solution)/shard_map/ppermute | solution.py:890
  138.1 72.5 %collective-permute-start.17 = (bf16[448,384]{1,0:T(8,128)(2,1)}, bf16[448,384]{1,0:T(8,128)(2,1)S(1)}, u32[]{:S(2)}, u32[]{:S(2)}) collective-permute-start(bf16[448,384]{1,0:T(8,128)(2,1)} %get-tuple-element.150), channel_id=1, source_target_pairs={{0,4},{2,6},{4,0},{6,2},{8,12},{10,14},{12,8},{14,10},{16,20},{18,... | collective-permute-start | bytes 1032200 | tf_op jit(solution)/shard_map/ppermute | solution.py:890
  210.6 12.5 %attention1.1 = (bf16[16,72,384]{2,1,0:T(8,128)(2,1)}, bf16[16,72,384]{2,1,0:T(8,128)(2,1)}, bf16[1024,384]{1,0:T(8,128)(2,1)}, bf16[1024,384]{1,0:T(8,128)(2,1)}) custom-call(s32[8]{0:T(128)} %get-tuple-element.102.refs_0_, s32[8,16]{1,0:T(8,128)} %get-tuple-element.103.refs_1_, bf16[32,72,384]{2,1,0:T(8,128)(2,1)} %refs_2_.5, ...), custom_call_target="tpu_custom_call" | custom-call | flops 127401984 | bytes 221184 | tf_op jit(solution)/shard_map/attention1/pallas_call | solution.py:783
  223.1 4.7 %collective-permute-done.17.refs_2_ = bf16[448,384]{1,0:T(8,128)(2,1)S(1)} collective-permute-done((bf16[448,384]{1,0:T(8,128)(2,1)}, bf16[448,384]{1,0:T(8,128)(2,1)S(1)}, u32[]{:S(2)}, u32[]{:S(2)}) %collective-permute-start.17) | collective-permute-done | bytes 344096 | tf_op jit(solution)/shard_map/ppermute | solution.py:890
  227.8 3.0 collective-permute-done.18.refs_3_
  231.2 2.0 collective-permute-done.19.refs_5_
  234.1 3.0 fold.6
  237.1 15.7 %collective-permute-start.20 = (bf16[112,384]{1,0:T(8,128)(2,1)}, bf16[112,384]{1,0:T(8,128)(2,1)S(1)}, u32[]{:S(2)}, u32[]{:S(2)}) collective-permute-start(bf16[112,384]{1,0:T(8,128)(2,1)} %get-tuple-element.159), channel_id=1, source_target_pairs={{0,8},{2,10},{4,12},{6,14},{8,0},{10,2},{12,4},{14,6},{16,24},{18,... | collective-permute-start | bytes 258056 | tf_op jit(solution)/shard_map/ppermute | solution.py:890
  252.8 2.4 collective-permute-start.22
  255.2 1.2 collective-permute-done.20.refs_1_
  256.8 5.0 %collective-permute-done.21.refs_2_ = bf16[112,384]{1,0:T(8,128)(2,1)S(1)} collective-permute-done((bf16[112,384]{1,0:T(8,128)(2,1)}, bf16[112,384]{1,0:T(8,128)(2,1)S(1)}, u32[]{:S(2)}, u32[]{:S(2)}) %collective-permute-start.21) | collective-permute-done | bytes 86048 | tf_op jit(solution)/shard_map/ppermute | solution.py:890
  261.8 2.3 collective-permute-start.24
  265.0 8.0 %collective-permute-done.24.refs_6_ = bf16[256,384]{1,0:T(8,128)(2,1)S(1)} collective-permute-done((bf16[256,384]{1,0:T(8,128)(2,1)}, bf16[256,384]{1,0:T(8,128)(2,1)S(1)}, u32[]{:S(2)}, u32[]{:S(2)}) %collective-permute-start.24) | collective-permute-done | bytes 196640 | tf_op jit(solution)/shard_map/ppermute | solution.py:890
  273.8 2.1 fold.7
  275.9 1.9 collective-permute-start.30
  277.8 2.5 collective-permute-start.31
  280.3 1.6 collective-permute-done.30.refs_6_
  281.9 1.7 collective-permute-start.27
  284.0 3.1 collective-permute-start.28
  287.1 4.9 %collective-permute-done.27.refs_2_ = bf16[112,384]{1,0:T(8,128)(2,1)S(1)} collective-permute-done((bf16[112,384]{1,0:T(8,128)(2,1)}, bf16[112,384]{1,0:T(8,128)(2,1)S(1)}, u32[]{:S(2)}, u32[]{:S(2)}) %collective-permute-start.27) | collective-permute-done | bytes 86048 | tf_op jit(solution)/shard_map/ppermute | solution.py:890
  292.7 1.9 fold.8
  294.5 1.8 collective-permute-start.35
  296.9 2.1 collective-permute-start.37
  298.9 0.9 collective-permute-done.35.refs_1_
  299.9 1.9 collective-permute-done.36.refs_2_
  301.7 1.2 collective-permute-done.37.refs_3_
  303.6 1.6 fold.9.refs_4_
  305.2 2.9 collective-permute-start.38
  308.2 3.4 collective-permute-start.34
  311.7 2.4 collective-permute-done.38.refs_5_
  314.9 4.3 %settle.1 = (bf16[32,72,384]{2,1,0:T(8,128)(2,1)}, bf16[32,72,384]{2,1,0:T(8,128)(2,1)}) custom-call(s32[2,32]{1,0:T(2,128)} %get-tuple-element.101.place, bf16[16,72,384]{2,1,0:T(8,128)(2,1)} %get-tuple-element.141.refs_0_, bf16[16,72,384]{2,1,0:T(8,128)(2,1)} %copy-done.6, bf16[16,72,384]{2,1,0:T(8,128)(2,1)} %get-tuple-element.143.refs_2_, ...), custom_call_target="tpu_custom_call" | custom-call | tf_op jit(solution)/shard_map/settle/pallas_call | solution.py:847
  319.2 29.1 %all-reduce.2.cloned.1.call-done.refs_8_ = bf16[2816,384]{1,0:T(8,128)(2,1)} async-done(((bf16[2816,384]{1,0:T(8,128)(2,1)}), bf16[2816,384]{1,0:T(8,128)(2,1)}) %all-reduce.2.cloned.1.call-update) | async-done | bytes 2162704 | tf_op jit(solution)/shard_map/psum | solution.py:1138
  350.0 6.3 %unpack.1 = (f32[2,384,768]{2,1,0:T(8,128)}, f32[2,768,384]{2,1,0:T(8,128)}, f32[2,3,192,384]{3,2,1,0:T(8,128)}, f32[2,192,384]{2,1,0:T(8,128)}, f32[2,6,144,144...) custom-call(s32[1]{0:T(128)} %bitcast.2.digit_ref, ...), custom_call_target="tpu_custom_call" | custom-call | tf_op jit(solution)/shard_map/unpack/pallas_call | solution.py:1039
  (126 shorter events, 15.8 us)
Async XLA Ops:
  7.2 341.2 %all-reduce.2.cloned.1.call-start = ((), (), s32[]{:S(2)}) async-start(), calls=%async_computation | async-start | bytes 4325376 | tf_op jit(solution)/shard_map/psum | solution.py:1138
  7.2 10.2 %collective-permute-start.1 = (bf16[2,3,192,384]{3,2,1,0:T(8,128)(2,1)}, bf16[2,3,192,384]{3,2,1,0:T(8,128)(2,1)S(1)}, u32[]{:S(2)}, u32[]{:S(2)}) collective-permute-start(bf16[2,3,192,384]{3,2,1,0:T(8,128)(2,1)} %bitcast.5), channel_id=1, source_target_pairs={{0,1},{1,0},{2,3},{3,2},{4,5},{5,4},{6,7},{7,6},{8,9},{9,8},{10,11... | collective-permute-start | bytes 2654216 | tf_op jit(solution)/shard_map/ppermute | solution.py:1053
  7.7 16.6 %collective-permute-start = (bf16[32,72,384]{2,1,0:T(8,128)(2,1)}, bf16[32,72,384]{2,1,0:T(8,128)(2,1)S(1)}, u32[]{:S(2)}, u32[]{:S(2)}) collective-permute-start(bf16[32,72,384]{2,1,0:T(8,128)(2,1)} %refs_2_.5), channel_id=1, source_target_pairs={{0,1},{1,0},{2,3},{3,2},{4,5},{5,4},{6,7},{7,6},{8,9},{9,8},{10,11... | collective-permute-start | bytes 5308424 | tf_op jit(solution)/shard_map/ppermute | solution.py:1053
  7.8 35.8 %collective-permute-start.9 = (bf16[32,72,384]{2,1,0:T(8,128)(2,1)}, bf16[32,72,384]{2,1,0:T(8,128)(2,1)}, u32[]{:S(2)}, u32[]{:S(2)}) collective-permute-start(bf16[32,72,384]{2,1,0:T(8,128)(2,1)} %refs_4_.5), channel_id=1, source_target_pairs={{0,1},{1,0},{2,3},{3,2},{4,5},{5,4},{6,7},{7,6},{8,9},{9,8},{10,11... | collective-permute-start | bytes 5308424 | tf_op jit(solution)/shard_map/ppermute | solution.py:1053
  8.3 9.0 %collective-permute-start.5 = (bf16[2,192,384]{2,1,0:T(8,128)(2,1)}, bf16[2,192,384]{2,1,0:T(8,128)(2,1)S(1)}, u32[]{:S(2)}, u32[]{:S(2)}) collective-permute-start(bf16[2,192,384]{2,1,0:T(8,128)(2,1)} %refs_8_.5), channel_id=1, source_target_pairs={{0,1},{1,0},{2,3},{3,2},{4,5},{5,4},{6,7},{7,6},{8,9},{9,8},{10,11... | collective-permute-start | bytes 884744 | tf_op jit(solution)/shard_map/ppermute | solution.py:1053
  8.3 7.2 %collective-permute-start.3 = (f32[2,2,192]{2,1,0:T(2,128)}, f32[2,2,192]{2,1,0:T(2,128)S(1)}, u32[]{:S(2)}, u32[]{:S(2)}) collective-permute-start(f32[2,2,192]{2,1,0:T(2,128)} %refs_11_.3), channel_id=1, source_target_pairs={{0,1},{1,0},{2,3},{3,2},{4,5},{5,4},{6,7},{7,6},{8,9},{9,8},{10,11... | collective-permute-start | bytes 9224 | tf_op jit(solution)/shard_map/ppermute | solution.py:1053
  15.5 1.4 collective-permute-start.4
  16.9 7.4 %collective-permute-start.6 = (bf16[2,384,768]{2,1,0:T(8,128)(2,1)}, bf16[2,384,768]{2,1,0:T(8,128)(2,1)}, u32[]{:S(2)}, u32[]{:S(2)}) collective-permute-start(bf16[2,384,768]{2,1,0:T(8,128)(2,1)} %refs_10_.3), channel_id=1, source_target_pairs={{0,1},{1,0},{2,3},{3,2},{4,5},{5,4},{6,7},{7,6},{8,9},{9,8},{10,11... | collective-permute-start | bytes 3538952 | tf_op jit(solution)/shard_map/ppermute | solution.py:1053
  17.3 7.1 %collective-permute-start.7 = (bf16[2,768,384]{2,1,0:T(8,128)(2,1)}, bf16[2,768,384]{2,1,0:T(8,128)(2,1)}, u32[]{:S(2)}, u32[]{:S(2)}) collective-permute-start(bf16[2,768,384]{2,1,0:T(8,128)(2,1)} %refs_12_.1), channel_id=1, source_target_pairs={{0,1},{1,0},{2,3},{3,2},{4,5},{5,4},{6,7},{7,6},{8,9},{9,8},{10,11... | collective-permute-start | bytes 3538952 | tf_op jit(solution)/shard_map/ppermute | solution.py:1053
  17.4 6.9 %collective-permute-start.2 = (f32[2,6,144,144]{3,2,1,0:T(8,128)}, f32[2,6,144,144]{3,2,1,0:T(8,128)}, u32[]{:S(2)}, u32[]{:S(2)}) collective-permute-start(f32[2,6,144,144]{3,2,1,0:T(8,128)} %refs_6_.4), channel_id=1, source_target_pairs={{0,1},{1,0},{2,3},{3,2},{4,5},{5,4},{6,7},{7,6},{8,9},{9,8},{10,11... | collective-permute-start | bytes 2985992 | tf_op jit(solution)/shard_map/ppermute | solution.py:1053
  43.3 1.5 collective-permute-start.8
  60.9 15.6 %collective-permute-start.10 = (bf16[1792,384]{1,0:T(8,128)(2,1)}, bf16[1792,384]{1,0:T(8,128)(2,1)S(1)}, u32[]{:S(2)}, u32[]{:S(2)}) collective-permute-start(bf16[1792,384]{1,0:T(8,128)(2,1)} %get-tuple-element.116), channel_id=1, source_target_pairs={{0,1},{1,0},{2,3},{3,2},{4,5},{5,4},{6,7},{7,6},{8,9},{9,8},{10,11... | collective-permute-start | bytes 4128776 | tf_op jit(solution)/shard_map/ppermute | solution.py:1053
  73.9 2.6 collective-permute-start.11
  74.1 7.7 %collective-permute-start.12 = (bf16[72,384]{1,0:T(8,128)(2,1)}, bf16[72,384]{1,0:T(8,128)(2,1)S(1)}, u32[]{:S(2)}, u32[]{:S(2)}) collective-permute-start(bf16[72,384]{1,0:T(8,128)(2,1)} %get-tuple-element.119), channel_id=1, source_target_pairs={{0,1},{1,0},{2,3},{3,2},{4,5},{5,4},{6,7},{7,6},{8,9},{9,8},{10,11... | collective-permute-start | bytes 165896 | tf_op jit(solution)/shard_map/ppermute | solution.py:1053
  95.7 3.4 collective-permute-start.13
  103.1 120.0 %collective-permute-start.16 = (bf16[448,384]{1,0:T(8,128)(2,1)}, bf16[448,384]{1,0:T(8,128)(2,1)S(1)}, u32[]{:S(2)}, u32[]{:S(2)}) collective-permute-start(bf16[448,384]{1,0:T(8,128)(2,1)} %get-tuple-element.149), channel_id=1, source_target_pairs={{0,2},{2,0},{4,6},{6,4},{8,10},{10,8},{12,14},{14,12},{16,18},{18,... | collective-permute-start | bytes 1032200 | tf_op jit(solution)/shard_map/ppermute | solution.py:890
  138.1 89.7 %collective-permute-start.17 = (bf16[448,384]{1,0:T(8,128)(2,1)}, bf16[448,384]{1,0:T(8,128)(2,1)S(1)}, u32[]{:S(2)}, u32[]{:S(2)}) collective-permute-start(bf16[448,384]{1,0:T(8,128)(2,1)} %get-tuple-element.150), channel_id=1, source_target_pairs={{0,4},{2,6},{4,0},{6,2},{8,12},{10,14},{12,8},{14,10},{16,20},{18,... | collective-permute-start | bytes 1032200 | tf_op jit(solution)/shard_map/ppermute | solution.py:890
  210.6 20.1 %collective-permute-start.18 = (bf16[448,384]{1,0:T(8,128)(2,1)}, bf16[448,384]{1,0:T(8,128)(2,1)S(1)}, u32[]{:S(2)}, u32[]{:S(2)}) collective-permute-start(bf16[448,384]{1,0:T(8,128)(2,1)} %get-tuple-element.151), channel_id=1, source_target_pairs={{0,6},{2,4},{4,2},{6,0},{8,14},{10,12},{12,10},{14,8},{16,22},{18,... | collective-permute-start | bytes 1032200 | tf_op jit(solution)/shard_map/ppermute | solution.py:890
  223.1 10.2 %copy-start.9 = (bf16[448,384]{1,0:T(8,128)(2,1)}, bf16[448,384]{1,0:T(8,128)(2,1)S(1)}, u32[]{:S(2)}) copy-start(bf16[448,384]{1,0:T(8,128)(2,1)S(1)} %collective-permute-done.16.refs_1_) | copy-start | bytes 1032196
  230.7 2.5 collective-permute-start.19
  230.7 77.4 %collective-permute-start.15 = (bf16[16,72,384]{2,1,0:T(8,128)(2,1)}, bf16[16,72,384]{2,1,0:T(8,128)(2,1)S(1)}, u32[]{:S(2)}, u32[]{:S(2)}) collective-permute-start(bf16[16,72,384]{2,1,0:T(8,128)(2,1)} %get-tuple-element.144), channel_id=1, source_target_pairs={{0,1},{1,0},{2,3},{3,2},{4,5},{5,4},{6,7},{7,6},{8,9},{9,8},{10,11... | collective-permute-start | bytes 2654216 | tf_op jit(solution)/shard_map/ppermute | solution.py:1053
  231.2 80.4 %collective-permute-start.14 = (bf16[16,72,384]{2,1,0:T(8,128)(2,1)}, bf16[16,72,384]{2,1,0:T(8,128)(2,1)S(1)}, u32[]{:S(2)}, u32[]{:S(2)}) collective-permute-start(bf16[16,72,384]{2,1,0:T(8,128)(2,1)} %get-tuple-element.142), channel_id=1, source_target_pairs={{0,1},{1,0},{2,3},{3,2},{4,5},{5,4},{6,7},{7,6},{8,9},{9,8},{10,11... | collective-permute-start | bytes 2654216 | tf_op jit(solution)/shard_map/ppermute | solution.py:1053
  237.1 19.3 %collective-permute-start.20 = (bf16[112,384]{1,0:T(8,128)(2,1)}, bf16[112,384]{1,0:T(8,128)(2,1)S(1)}, u32[]{:S(2)}, u32[]{:S(2)}) collective-permute-start(bf16[112,384]{1,0:T(8,128)(2,1)} %get-tuple-element.159), channel_id=1, source_target_pairs={{0,8},{2,10},{4,12},{6,14},{8,0},{10,2},{12,4},{14,6},{16,24},{18,... | collective-permute-start | bytes 258056 | tf_op jit(solution)/shard_map/ppermute | solution.py:890
  252.8 9.0 %collective-permute-start.21 = (bf16[112,384]{1,0:T(8,128)(2,1)}, bf16[112,384]{1,0:T(8,128)(2,1)S(1)}, u32[]{:S(2)}, u32[]{:S(2)}) collective-permute-start(bf16[112,384]{1,0:T(8,128)(2,1)} %get-tuple-element.160), channel_id=1, source_target_pairs={{0,16},{2,18},{4,20},{6,22},{8,24},{10,26},{12,28},{14,30},{16,0},... | collective-permute-start | bytes 258056 | tf_op jit(solution)/shard_map/ppermute | solution.py:890
  252.8 11.3 %collective-permute-start.22 = (bf16[112,384]{1,0:T(8,128)(2,1)}, bf16[112,384]{1,0:T(8,128)(2,1)S(1)}, u32[]{:S(2)}, u32[]{:S(2)}) collective-permute-start(bf16[112,384]{1,0:T(8,128)(2,1)} %get-tuple-element.161), channel_id=1, source_target_pairs={{0,24},{2,26},{4,28},{6,30},{8,16},{10,18},{12,20},{14,22},{16,8},... | collective-permute-start | bytes 258056 | tf_op jit(solution)/shard_map/ppermute | solution.py:890
  256.4 16.6 %copy-start.25 = (bf16[112,384]{1,0:T(8,128)(2,1)}, bf16[112,384]{1,0:T(8,128)(2,1)S(1)}, u32[]{:S(2)}) copy-start(bf16[112,384]{1,0:T(8,128)(2,1)S(1)} %collective-permute-done.20.refs_1_) | copy-start | bytes 258052
  256.4 8.6 %collective-permute-start.23 = (bf16[256,384]{1,0:T(8,128)(2,1)}, bf16[256,384]{1,0:T(8,128)(2,1)S(1)}, u32[]{:S(2)}, u32[]{:S(2)}) collective-permute-start(bf16[256,384]{1,0:T(8,128)(2,1)} %get-tuple-element.163), channel_id=1, source_target_pairs={{0,2},{2,0},{4,6},{6,4},{8,10},{10,8},{12,14},{14,12},{16,18},{18,... | collective-permute-start | bytes 589832 | tf_op jit(solution)/shard_map/ppermute | solution.py:890
  261.8 11.3 %copy-start.26 = (bf16[112,384]{1,0:T(8,128)(2,1)}, bf16[112,384]{1,0:T(8,128)(2,1)S(1)}, u32[]{:S(2)}) copy-start(bf16[112,384]{1,0:T(8,128)(2,1)S(1)} %collective-permute-done.21.refs_2_) | copy-start | bytes 258052
  261.8 11.2 %collective-permute-start.24 = (bf16[256,384]{1,0:T(8,128)(2,1)}, bf16[256,384]{1,0:T(8,128)(2,1)S(1)}, u32[]{:S(2)}, u32[]{:S(2)}) collective-permute-start(bf16[256,384]{1,0:T(8,128)(2,1)} %get-tuple-element.164), channel_id=1, source_target_pairs={{0,4},{2,6},{4,0},{6,2},{8,12},{10,14},{12,8},{14,10},{16,20},{18,... | collective-permute-start | bytes 589832 | tf_op jit(solution)/shard_map/ppermute | solution.py:890
  264.1 9.0 %copy-start.27 = (bf16[112,384]{1,0:T(8,128)(2,1)}, bf16[112,384]{1,0:T(8,128)(2,1)S(1)}, u32[]{:S(2)}) copy-start(bf16[112,384]{1,0:T(8,128)(2,1)S(1)} %collective-permute-done.22.refs_3_) | copy-start | bytes 258052
  264.1 9.0 %collective-permute-start.25 = (bf16[256,384]{1,0:T(8,128)(2,1)}, bf16[256,384]{1,0:T(8,128)(2,1)S(1)}, u32[]{:S(2)}, u32[]{:S(2)}) collective-permute-start(bf16[256,384]{1,0:T(8,128)(2,1)} %get-tuple-element.165), channel_id=1, source_target_pairs={{0,6},{2,4},{4,2},{6,0},{8,14},{10,12},{12,10},{14,8},{16,22},{18,... | collective-permute-start | bytes 589832 | tf_op jit(solution)/shard_map/ppermute | solution.py:890
  275.9 4.4 %collective-permute-start.29 = (bf16[64,384]{1,0:T(8,128)(2,1)}, bf16[64,384]{1,0:T(8,128)(2,1)S(1)}, u32[]{:S(2)}, u32[]{:S(2)}) collective-permute-start(bf16[64,384]{1,0:T(8,128)(2,1)} %get-tuple-element.168), channel_id=1, source_target_pairs={{0,8},{2,10},{4,12},{6,14},{8,0},{10,2},{12,4},{14,6},{16,24},{18,... | collective-permute-start | bytes 147464 | tf_op jit(solution)/shard_map/ppermute | solution.py:890
  275.9 6.0 %collective-permute-start.30 = (bf16[64,384]{1,0:T(8,128)(2,1)}, bf16[64,384]{1,0:T(8,128)(2,1)S(1)}, u32[]{:S(2)}, u32[]{:S(2)}) collective-permute-start(bf16[64,384]{1,0:T(8,128)(2,1)} %get-tuple-element.169), channel_id=1, source_target_pairs={{0,16},{2,18},{4,20},{6,22},{8,24},{10,26},{12,28},{14,30},{16,0},... | collective-permute-start | bytes 147464 | tf_op jit(solution)/shard_map/ppermute | solution.py:890
  277.8 6.2 %collective-permute-start.31 = (bf16[64,384]{1,0:T(8,128)(2,1)}, bf16[64,384]{1,0:T(8,128)(2,1)S(1)}, u32[]{:S(2)}, u32[]{:S(2)}) collective-permute-start(bf16[64,384]{1,0:T(8,128)(2,1)} %get-tuple-element.170), channel_id=1, source_target_pairs={{0,24},{2,26},{4,28},{6,30},{8,16},{10,18},{12,20},{14,22},{16,8},... | collective-permute-start | bytes 147464 | tf_op jit(solution)/shard_map/ppermute | solution.py:890
  280.3 11.7 %copy-start.29 = (bf16[64,384]{1,0:T(8,128)(2,1)}, bf16[64,384]{1,0:T(8,128)(2,1)S(1)}, u32[]{:S(2)}) copy-start(bf16[64,384]{1,0:T(8,128)(2,1)S(1)} %collective-permute-done.29.refs_5_) | copy-start | bytes 147460
  280.3 6.8 %collective-permute-start.26 = (bf16[112,384]{1,0:T(8,128)(2,1)}, bf16[112,384]{1,0:T(8,128)(2,1)S(1)}, u32[]{:S(2)}, u32[]{:S(2)}) collective-permute-start(bf16[112,384]{1,0:T(8,128)(2,1)} %get-tuple-element.166.refs_0_), channel_id=1, source_target_pairs={{0,8},{2,10},{4,12},{6,14},{8,0},{10,2},{12,4},{14,6},{16,24},{18,... | collective-permute-start | bytes 258056 | tf_op jit(solution)/shard_map/ppermute | solution.py:890
  281.9 10.2 %copy-start.30 = (bf16[64,384]{1,0:T(8,128)(2,1)}, bf16[64,384]{1,0:T(8,128)(2,1)S(1)}, u32[]{:S(2)}) copy-start(bf16[64,384]{1,0:T(8,128)(2,1)S(1)} %collective-permute-done.30.refs_6_) | copy-start | bytes 147460
  281.9 10.1 %collective-permute-start.27 = (bf16[112,384]{1,0:T(8,128)(2,1)}, bf16[112,384]{1,0:T(8,128)(2,1)S(1)}, u32[]{:S(2)}, u32[]{:S(2)}) collective-permute-start(bf16[112,384]{1,0:T(8,128)(2,1)} %get-tuple-element.166.refs_0_), channel_id=1, source_target_pairs={{0,16},{2,18},{4,20},{6,22},{8,24},{10,26},{12,28},{14,30},{16,0},... | collective-permute-start | bytes 258056 | tf_op jit(solution)/shard_map/ppermute | solution.py:890
  284.0 8.0 %collective-permute-start.28 = (bf16[112,384]{1,0:T(8,128)(2,1)}, bf16[112,384]{1,0:T(8,128)(2,1)S(1)}, u32[]{:S(2)}, u32[]{:S(2)}) collective-permute-start(bf16[112,384]{1,0:T(8,128)(2,1)} %get-tuple-element.166.refs_0_), channel_id=1, source_target_pairs={{0,24},{2,26},{4,28},{6,30},{8,16},{10,18},{12,20},{14,22},{16,8},... | collective-permute-start | bytes 258056 | tf_op jit(solution)/shard_map/ppermute | solution.py:890
  294.5 5.3 %collective-permute-start.35 = (bf16[64,384]{1,0:T(8,128)(2,1)}, bf16[64,384]{1,0:T(8,128)(2,1)S(1)}, u32[]{:S(2)}, u32[]{:S(2)}) collective-permute-start(bf16[64,384]{1,0:T(8,128)(2,1)} %get-tuple-element.172.refs_0_), channel_id=1, source_target_pairs={{0,8},{2,10},{4,12},{6,14},{8,0},{10,2},{12,4},{14,6},{16,24},{18,... | collective-permute-start | bytes 147464 | tf_op jit(solution)/shard_map/ppermute | solution.py:890
  296.3 5.4 %collective-permute-start.36 = (bf16[64,384]{1,0:T(8,128)(2,1)}, bf16[64,384]{1,0:T(8,128)(2,1)S(1)}, u32[]{:S(2)}, u32[]{:S(2)}) collective-permute-start(bf16[64,384]{1,0:T(8,128)(2,1)} %get-tuple-element.172.refs_0_), channel_id=1, source_target_pairs={{0,16},{2,18},{4,20},{6,22},{8,24},{10,26},{12,28},{14,30},{16,0},... | collective-permute-start | bytes 147464 | tf_op jit(solution)/shard_map/ppermute | solution.py:890
  296.9 6.1 %collective-permute-start.37 = (bf16[64,384]{1,0:T(8,128)(2,1)}, bf16[64,384]{1,0:T(8,128)(2,1)S(1)}, u32[]{:S(2)}, u32[]{:S(2)}) collective-permute-start(bf16[64,384]{1,0:T(8,128)(2,1)} %get-tuple-element.172.refs_0_), channel_id=1, source_target_pairs={{0,24},{2,26},{4,28},{6,30},{8,16},{10,18},{12,20},{14,22},{16,8},... | collective-permute-start | bytes 147464 | tf_op jit(solution)/shard_map/ppermute | solution.py:890
  305.2 8.9 %collective-permute-start.38 = (bf16[256,384]{1,0:T(8,128)(2,1)}, bf16[256,384]{1,0:T(8,128)(2,1)S(1)}, u32[]{:S(2)}, u32[]{:S(2)}) collective-permute-start(bf16[256,384]{1,0:T(8,128)(2,1)} %fold.9.refs_4_), channel_id=1, source_target_pairs={{0,2},{2,0},{4,6},{6,4},{8,10},{10,8},{12,14},{14,12},{16,18},{18,... | collective-permute-start | bytes 589832 | tf_op jit(solution)/shard_map/ppermute | solution.py:890
  308.1 40.3 %collective-permute-start.32 = (bf16[448,384]{1,0:T(8,128)(2,1)}, bf16[448,384]{1,0:T(8,128)(2,1)S(1)}, u32[]{:S(2)}, u32[]{:S(2)}) collective-permute-start(bf16[448,384]{1,0:T(8,128)(2,1)} %get-tuple-element.171.refs_0_), channel_id=1, source_target_pairs={{0,2},{2,0},{4,6},{6,4},{8,10},{10,8},{12,14},{14,12},{16,18},{18,... | collective-permute-start | bytes 1032200 | tf_op jit(solution)/shard_map/ppermute | solution.py:890
  308.1 40.2 %collective-permute-start.33 = (bf16[448,384]{1,0:T(8,128)(2,1)}, bf16[448,384]{1,0:T(8,128)(2,1)S(1)}, u32[]{:S(2)}, u32[]{:S(2)}) collective-permute-start(bf16[448,384]{1,0:T(8,128)(2,1)} %get-tuple-element.171.refs_0_), channel_id=1, source_target_pairs={{0,4},{2,6},{4,0},{6,2},{8,12},{10,14},{12,8},{14,10},{16,20},{18,... | collective-permute-start | bytes 1032200 | tf_op jit(solution)/shard_map/ppermute | solution.py:890
  308.2 40.3 %collective-permute-start.34 = (bf16[448,384]{1,0:T(8,128)(2,1)}, bf16[448,384]{1,0:T(8,128)(2,1)S(1)}, u32[]{:S(2)}, u32[]{:S(2)}) collective-permute-start(bf16[448,384]{1,0:T(8,128)(2,1)} %get-tuple-element.171.refs_0_), channel_id=1, source_target_pairs={{0,6},{2,4},{4,2},{6,0},{8,14},{10,12},{12,10},{14,8},{16,22},{18,... | collective-permute-start | bytes 1032200 | tf_op jit(solution)/shard_map/ppermute | solution.py:890
  311.6 36.7 %collective-permute-start.39 = (bf16[256,384]{1,0:T(8,128)(2,1)}, bf16[256,384]{1,0:T(8,128)(2,1)S(1)}, u32[]{:S(2)}, u32[]{:S(2)}) collective-permute-start(bf16[256,384]{1,0:T(8,128)(2,1)} %fold.9.refs_4_), channel_id=1, source_target_pairs={{0,4},{2,6},{4,0},{6,2},{8,12},{10,14},{12,8},{14,10},{16,20},{18,... | collective-permute-start | bytes 589832 | tf_op jit(solution)/shard_map/ppermute | solution.py:890
  314.1 34.2 %collective-permute-start.40 = (bf16[256,384]{1,0:T(8,128)(2,1)}, bf16[256,384]{1,0:T(8,128)(2,1)S(1)}, u32[]{:S(2)}, u32[]{:S(2)}) collective-permute-start(bf16[256,384]{1,0:T(8,128)(2,1)} %fold.9.refs_4_), channel_id=1, source_target_pairs={{0,6},{2,4},{4,2},{6,0},{8,14},{10,12},{12,10},{14,8},{16,22},{18,... | collective-permute-start | bytes 589832 | tf_op jit(solution)/shard_map/ppermute | solution.py:890
  (31 other events, 80.7 us)
Sparse Core Ops, SparseCore 0:
  96.0 252.2 all-reduce.1

commit v2 on v1

--- a/solution.py
+++ b/solution.py
@@ -890,21 +890,20 @@
     return lax.ppermute(value, DP, [(d, d ^ (k * stride)) for d in range(devices)])
 
 
-def stack_kernel(*refs):
+def stack_kernel(counts, *refs):
     out, pairs = refs[-1], refs[:-1]
     at = 0
-    for one, other in zip(pairs[0::2], pairs[1::2]):
-        rows = one.shape[0]
-        out[at : at + rows, :] = (one[...].astype(F32) + other[...].astype(F32)).astype(BF16)
+    for at_pair, (one, other) in enumerate(zip(pairs[0::2], pairs[1::2])):
+        rows = counts[at_pair]
+        out[at : at + rows, :] = (one[:rows].astype(F32) + other[:rows].astype(F32)).astype(BF16)
         at += rows
 
 
-def stack(*pairs):
+def stack(counts, *pairs):
     vmem = pl.BlockSpec(memory_space=pltpu.VMEM)
-    rows = sum(pair[0].shape[0] for pair in pairs)
     return pl.pallas_call(
-        stack_kernel,
-        out_shape=jax.ShapeDtypeStruct((rows, pairs[0][0].shape[1]), BF16),
+        functools.partial(stack_kernel, counts),
+        out_shape=jax.ShapeDtypeStruct((sum(counts), pairs[0][0].shape[1]), BF16),
         in_specs=[vmem] * (2 * len(pairs)),
         out_specs=vmem,
         compiler_params=pltpu.CompilerParams(vmem_limit_bytes=VMEM_LIMIT),
@@ -991,7 +990,7 @@
     part = width // 2
     win = earth.shape[2]
     third = win // 3
-    split = joined[0].shape[0]
+    split = 2 * hidden_part + part
     packs = [(joined[0], 0, joined[1], 0), (whole_two, 0, whole_two, split)]
     for b, (pack, base, other, base_other) in enumerate(packs):
         for at in range(0, hidden_part, width):
@@ -1133,7 +1132,8 @@
     recv_b = across(mixer_two.send)
     attention_two = run((False, False, True), 1, mixer_two, second)
     half_far = across(attention_two.out_half)
-    pack_two = stack((mixer_two.pack_own, pack_far), (attention_two.pack_own, across(attention_two.pack_oth)))
+    filled = (2 * hidden_part + width // 2, pack_rows(width, own_heads, win).total)
+    pack_two = stack(filled, (mixer_two.pack_own, pack_far), (attention_two.pack_own, across(attention_two.pack_oth)))
     pack_two, half_far = lax.optimization_barrier((pack_two, half_far))
     sum_two = lax.psum(pack_two, DP)
     back = Bag(grad_src=attention_two.out, grad_oth=half_far)

time: 370 us -> 368 us (level)
  Pallas kernels: 101 us -> 193 us
  starting transfers between devices: 155 us -> 72.4 us
  waiting for transfers between devices: 82.8 us -> 71.4 us
    pallas_call x5, Pallas kernels: 71.4 us -> 163 us  [run_block(): pl.pallas_call(functools.partial(block_kernel, [*ins, *outs, *scratch], s...]
    ppermute x24, starting transfers between devices: 150 us -> 67.3 us  [with_peer(): lax.ppermute(value, DP, [(d, d ^ k * stride) for d in range(devices)])]
    ppermute x24, waiting for transfers between devices: 35.3 us -> 27.1 us  [with_peer(): lax.ppermute(value, DP, [(d, d ^ k * stride) for d in range(devices)])]
  transfers between devices with their start and end apart: 42 -> 42, of which waited for: 20 -> 18; matrix products, arithmetic and copies ran while one was open for 0% -> 0% of each run, Pallas kernels for 18% -> 31%
where the time goes in v2:
time: 368 us; the launch traced here: 361 us
  Pallas kernels  193 us (52%)
  starting transfers between devices  72.4 us (20%)
  waiting for transfers between devices  71.4 us (19%)
  between operations  14.8 us (4%)
  local copies, waits for them, and re-layouts  9.4 us (3%)
    pallas_call x5, Pallas kernels, run_block(): pl.pallas_call(functools.partial(block_kernel, [*ins, *outs, *scratch], s...  163 us
    ppermute x24, starting transfers between devices, with_peer(): lax.ppermute(value, DP, [(d, d ^ k * stride) for d in range(devices)])  67.3 us
    ppermute x24, waiting for transfers between devices, with_peer(): lax.ppermute(value, DP, [(d, d ^ k * stride) for d in range(devices)])  27.1 us
    psum x1, waiting for transfers between devices, local(): sum_two = lax.psum(pack_two, DP)  26.5 us
    ppermute x17, waiting for transfers between devices, across(): return lax.ppermute(value, TENSOR, [(0, 1), (1, 0)])  17.8 us
    pallas_call x5, Pallas kernels, advance(): pl.pallas_call(functools.partial(local_kernel, jobs), out_shape=tuple((ja...  11.5 us
    unnamed x74, local copies, waits for them, and re-layouts  9.4 us
  transfers between devices with their start and end apart: 42, of which 18 were waited for; matrix products, arithmetic and copies ran while one was open for 0% of the time, Pallas kernels for 31%

profile of v2, /device:TPU:0, one launch (start us, length us, event | category | flops | bytes accessed | tf_op | source)
XLA Modules:
  0.0 361.2 jit_solution(16883332818463991936)
XLA Ops:
  8.8 6.7 %collective-permute-done.3.refs_10_.refs_12_ = f32[2,2,192]{2,1,0:T(2,128)S(1)} collective-permute-done((f32[2,2,192]{2,1,0:T(2,128)}, f32[2,2,192]{2,1,0:T(2,128)S(1)}, u32[]{:S(2)}, u32[]{:S(2)}) %collective-permute-start.3) | collective-permute-done | bytes 3104 | tf_op jit(solution)/shard_map/ppermute | solution.py:1052
  15.9 1.0 collective-permute-done.4.refs_12_.refs_14_
  17.8 4.1 %plan.1 = (s32[8]{0:T(128)}, s32[8,16]{1,0:T(8,128)}, s32[2,32]{1,0:T(2,128)}) custom-call(s32[1]{0:T(128)} %bitcast.t_ref, s32[32,144]{1,0:T(8,128)} %mask_ref.1, s32[32]{0:T(128)} %next_ref.1), custom_call_target="tpu_custom_call" | custom-call | flops 5000000000 | bytes 16777216 | tf_op jit(solution)/shard_map/plan/pallas_call | solution.py:147
  21.9 2.4 collective-permute-done.2.refs_5_.refs_7_
  24.3 1.2 copy-done
  25.5 34.6 %ahead1.1 = (bf16[2304,1152]{1,0:T(8,128)(2,1)}, bf16[16,12,144,144]{3,2,1,0:T(8,128)(2,1)}, bf16[2304,384]{1,0:T(8,128)(2,1)}, bf16[2304,384]{1,0:T(8,128)(2,1)...) custom-call(s32[8]{0:T(128)} %get-tuple-element.102.refs_0_, ...), custom_call_target="tpu_custom_call" | custom-call | flops 127401984 | bytes 221184 | tf_op jit(solution)/shard_map/ahead1/pallas_call | solution.py:783
  60.5 1.1 collective-permute-done.8.refs_3_
  62.3 49.1 %aheadmixer2.1 = (bf16[2304,1152]{1,0:T(8,128)(2,1)}, bf16[16,12,144,144]{3,2,1,0:T(8,128)(2,1)}, bf16[2304,384]{1,0:T(8,128)(2,1)}, bf16[2304,384]{1,0:T(8,128)...) custom-call(s32[8]{0:T(128)} %get-tuple-element.102.refs_0_, ...), custom_call_target="tpu_custom_call" | custom-call | flops 254803968 | bytes 442368 | tf_op jit(solution)/shard_map/aheadmixer2/pallas_call | solution.py:783
  111.7 26.3 %attention2.1 = (bf16[16,2,72,384]{3,2,1,0:T(8,128)(2,1)}, bf16[72,384]{1,0:T(8,128)(2,1)}, bf16[1024,384]{1,0:T(8,128)(2,1)}, bf16[1024,384]{1,0:T(8,128)(2,1)}) custom-call(s32[8]{0:T(128)} %get-tuple-element.102.refs_0_, s32[8,16]{1,0:T(8,128)} %get-tuple-element.103.refs_1_, bf16[16,2,72,384]{3,2,1,0:T(8,128)(2,1)} %get-tuple-element.104.refs_2_, ...), custom_call_target="tpu_custom_call" | custom-call | flops 127401984 | bytes 221184 | tf_op jit(solution)/shard_map/attention2/pallas_call | solution.py:783
  138.6 2.0 collective-permute-done.11.refs_3_
  141.9 4.0 %stack.13 = bf16[2656,384]{1,0:T(8,128)(2,1)} custom-call(bf16[1792,384]{1,0:T(8,128)(2,1)} %get-tuple-element.115.refs_0_, bf16[1792,384]{1,0:T(8,128)(2,1)} %copy-done.4, bf16[1024,384]{1,0:T(8,128)(2,1)} %get-tuple-element.117.refs_2_, bf16[1024,384]{1,0:T(8,128)(2,1)} %copy-done.7), custom_call_target="tpu_custom_call" | custom-call | tf_op jit(solution)/shard_map/stack/pallas_call | solution.py:904
  146.5 25.3 %mixer1.1 = (bf16[2304,384]{1,0:T(8,128)(2,1)}, bf16[2304,384]{1,0:T(8,128)(2,1)}, bf16[2304,384]{1,0:T(8,128)(2,1)}, bf16[1792,384]{1,0:T(8,128)(2,1)}, bf16[17...) custom-call(s32[8]{0:T(128)} %get-tuple-element.102.refs_0_, s32[8,16]{1,0:T(8,128)} %get-tuple-element.103.refs_1_, ...), custom_call_target="tpu_custom_call" | custom-call | flops 127401984 | bytes 221184 | tf_op jit(solution)/shard_map/mixer1/pallas_call | solution.py:783
  172.6 2.6 collective-permute-done.13.refs_1_
  175.2 1.1 copy-done.3
  176.3 3.0 fold.5
  179.2 29.8 %collective-permute-start.16 = (bf16[448,384]{1,0:T(8,128)(2,1)}, bf16[448,384]{1,0:T(8,128)(2,1)S(1)}, u32[]{:S(2)}, u32[]{:S(2)}) collective-permute-start(bf16[448,384]{1,0:T(8,128)(2,1)} %get-tuple-element.149), channel_id=1, source_target_pairs={{0,2},{2,0},{4,6},{6,4},{8,10},{10,8},{12,14},{14,12},{16,18},{18,... | collective-permute-start | bytes 1032200 | tf_op jit(solution)/shard_map/ppermute | solution.py:890
  209.0 1.5 collective-permute-start.18
  210.5 27.4 %attention1.1 = (bf16[16,72,384]{2,1,0:T(8,128)(2,1)}, bf16[16,72,384]{2,1,0:T(8,128)(2,1)}, bf16[1024,384]{1,0:T(8,128)(2,1)}, bf16[1024,384]{1,0:T(8,128)(2,1)}) custom-call(s32[8]{0:T(128)} %get-tuple-element.102.refs_0_, s32[8,16]{1,0:T(8,128)} %get-tuple-element.103.refs_1_, bf16[32,72,384]{2,1,0:T(8,128)(2,1)} %refs_2_.5, ...), custom_call_target="tpu_custom_call" | custom-call | flops 127401984 | bytes 221184 | tf_op jit(solution)/shard_map/attention1/pallas_call | solution.py:783
  238.6 1.9 collective-permute-done.19.refs_5_
  241.4 3.0 fold.6
  244.3 8.4 %collective-permute-start.20 = (bf16[112,384]{1,0:T(8,128)(2,1)}, bf16[112,384]{1,0:T(8,128)(2,1)S(1)}, u32[]{:S(2)}, u32[]{:S(2)}) collective-permute-start(bf16[112,384]{1,0:T(8,128)(2,1)} %get-tuple-element.159), channel_id=1, source_target_pairs={{0,8},{2,10},{4,12},{6,14},{8,0},{10,2},{12,4},{14,6},{16,24},{18,... | collective-permute-start | bytes 258056 | tf_op jit(solution)/shard_map/ppermute | solution.py:890
  252.7 2.4 collective-permute-start.22
  255.9 2.6 collective-permute-start.23
  258.6 3.1 collective-permute-done.21.refs_2_
  261.6 2.8 collective-permute-start.25
  264.5 8.3 %collective-permute-done.24.refs_6_ = bf16[256,384]{1,0:T(8,128)(2,1)S(1)} collective-permute-done((bf16[256,384]{1,0:T(8,128)(2,1)}, bf16[256,384]{1,0:T(8,128)(2,1)S(1)}, u32[]{:S(2)}, u32[]{:S(2)}) %collective-permute-start.24) | collective-permute-done | bytes 196640 | tf_op jit(solution)/shard_map/ppermute | solution.py:890
  273.5 2.1 fold.7
  275.6 1.1 collective-permute-start.30
  276.7 3.3 collective-permute-start.31
  280.1 1.8 collective-permute-done.30.refs_6_
  282.0 1.6 collective-permute-done.31.refs_7_
  283.6 3.0 collective-permute-start.28
  286.7 4.5 %collective-permute-done.27.refs_2_ = bf16[112,384]{1,0:T(8,128)(2,1)S(1)} collective-permute-done((bf16[112,384]{1,0:T(8,128)(2,1)}, bf16[112,384]{1,0:T(8,128)(2,1)S(1)}, u32[]{:S(2)}, u32[]{:S(2)}) %collective-permute-start.27) | collective-permute-done | bytes 86048 | tf_op jit(solution)/shard_map/ppermute | solution.py:890
  291.9 1.9 fold.8
  293.7 1.8 collective-permute-start.35
  295.5 1.1 collective-permute-start.36
  296.6 1.5 collective-permute-start.37
  298.1 0.9 collective-permute-done.35.refs_1_
  299.1 2.0 collective-permute-done.36.refs_2_
  301.0 1.6 collective-permute-done.37.refs_3_
  303.3 1.6 fold.9.refs_4_
  304.9 2.9 collective-permute-start.38
  307.8 3.4 collective-permute-start.34
  311.3 2.5 collective-permute-done.38.refs_5_
  313.8 1.3 collective-permute-start.40
  315.1 4.3 %settle.1 = (bf16[32,72,384]{2,1,0:T(8,128)(2,1)}, bf16[32,72,384]{2,1,0:T(8,128)(2,1)}) custom-call(s32[2,32]{1,0:T(2,128)} %get-tuple-element.101.place, bf16[16,72,384]{2,1,0:T(8,128)(2,1)} %get-tuple-element.141.refs_0_, bf16[16,72,384]{2,1,0:T(8,128)(2,1)} %copy-done.6, bf16[16,72,384]{2,1,0:T(8,128)(2,1)} %get-tuple-element.143.refs_2_, ...), custom_call_target="tpu_custom_call" | custom-call | tf_op jit(solution)/shard_map/settle/pallas_call | solution.py:847
  319.5 26.5 %all-reduce.2.cloned.1.call-done.refs_8_ = bf16[2656,384]{1,0:T(8,128)(2,1)} async-done(((bf16[2656,384]{1,0:T(8,128)(2,1)}), bf16[2656,384]{1,0:T(8,128)(2,1)}) %all-reduce.2.cloned.1.call-update) | async-done | bytes 2039824 | tf_op jit(solution)/shard_map/psum | solution.py:1138
  347.7 6.3 %unpack.1 = (f32[2,384,768]{2,1,0:T(8,128)}, f32[2,768,384]{2,1,0:T(8,128)}, f32[2,3,192,384]{3,2,1,0:T(8,128)}, f32[2,192,384]{2,1,0:T(8,128)}, f32[2,6,144,144...) custom-call(s32[1]{0:T(128)} %bitcast.2.digit_ref, ...), custom_call_target="tpu_custom_call" | custom-call | tf_op jit(solution)/shard_map/unpack/pallas_call | solution.py:1038
  (126 shorter events, 14.0 us)
Async XLA Ops:
  7.2 338.8 %all-reduce.2.cloned.1.call-start = ((), (), s32[]{:S(2)}) async-start(), calls=%async_computation | async-start | bytes 4079616 | tf_op jit(solution)/shard_map/psum | solution.py:1138
  7.2 10.2 %collective-permute-start.1 = (bf16[2,3,192,384]{3,2,1,0:T(8,128)(2,1)}, bf16[2,3,192,384]{3,2,1,0:T(8,128)(2,1)S(1)}, u32[]{:S(2)}, u32[]{:S(2)}) collective-permute-start(bf16[2,3,192,384]{3,2,1,0:T(8,128)(2,1)} %bitcast.5), channel_id=1, source_target_pairs={{0,1},{1,0},{2,3},{3,2},{4,5},{5,4},{6,7},{7,6},{8,9},{9,8},{10,11... | collective-permute-start | bytes 2654216 | tf_op jit(solution)/shard_map/ppermute | solution.py:1052
  7.7 16.6 %collective-permute-start = (bf16[32,72,384]{2,1,0:T(8,128)(2,1)}, bf16[32,72,384]{2,1,0:T(8,128)(2,1)S(1)}, u32[]{:S(2)}, u32[]{:S(2)}) collective-permute-start(bf16[32,72,384]{2,1,0:T(8,128)(2,1)} %refs_2_.5), channel_id=1, source_target_pairs={{0,1},{1,0},{2,3},{3,2},{4,5},{5,4},{6,7},{7,6},{8,9},{9,8},{10,11... | collective-permute-start | bytes 5308424 | tf_op jit(solution)/shard_map/ppermute | solution.py:1052
  7.8 52.7 %collective-permute-start.9 = (bf16[32,72,384]{2,1,0:T(8,128)(2,1)}, bf16[32,72,384]{2,1,0:T(8,128)(2,1)}, u32[]{:S(2)}, u32[]{:S(2)}) collective-permute-start(bf16[32,72,384]{2,1,0:T(8,128)(2,1)} %refs_4_.5), channel_id=1, source_target_pairs={{0,1},{1,0},{2,3},{3,2},{4,5},{5,4},{6,7},{7,6},{8,9},{9,8},{10,11... | collective-permute-start | bytes 5308424 | tf_op jit(solution)/shard_map/ppermute | solution.py:1052
  8.3 9.0 %collective-permute-start.5 = (bf16[2,192,384]{2,1,0:T(8,128)(2,1)}, bf16[2,192,384]{2,1,0:T(8,128)(2,1)S(1)}, u32[]{:S(2)}, u32[]{:S(2)}) collective-permute-start(bf16[2,192,384]{2,1,0:T(8,128)(2,1)} %refs_8_.5), channel_id=1, source_target_pairs={{0,1},{1,0},{2,3},{3,2},{4,5},{5,4},{6,7},{7,6},{8,9},{9,8},{10,11... | collective-permute-start | bytes 884744 | tf_op jit(solution)/shard_map/ppermute | solution.py:1052
  8.3 7.2 %collective-permute-start.3 = (f32[2,2,192]{2,1,0:T(2,128)}, f32[2,2,192]{2,1,0:T(2,128)S(1)}, u32[]{:S(2)}, u32[]{:S(2)}) collective-permute-start(f32[2,2,192]{2,1,0:T(2,128)} %refs_11_.3), channel_id=1, source_target_pairs={{0,1},{1,0},{2,3},{3,2},{4,5},{5,4},{6,7},{7,6},{8,9},{9,8},{10,11... | collective-permute-start | bytes 9224 | tf_op jit(solution)/shard_map/ppermute | solution.py:1052
  15.5 1.4 collective-permute-start.4
  16.9 7.4 %collective-permute-start.6 = (bf16[2,384,768]{2,1,0:T(8,128)(2,1)}, bf16[2,384,768]{2,1,0:T(8,128)(2,1)}, u32[]{:S(2)}, u32[]{:S(2)}) collective-permute-start(bf16[2,384,768]{2,1,0:T(8,128)(2,1)} %refs_10_.3), channel_id=1, source_target_pairs={{0,1},{1,0},{2,3},{3,2},{4,5},{5,4},{6,7},{7,6},{8,9},{9,8},{10,11... | collective-permute-start | bytes 3538952 | tf_op jit(solution)/shard_map/ppermute | solution.py:1052
  17.3 7.1 %collective-permute-start.7 = (bf16[2,768,384]{2,1,0:T(8,128)(2,1)}, bf16[2,768,384]{2,1,0:T(8,128)(2,1)}, u32[]{:S(2)}, u32[]{:S(2)}) collective-permute-start(bf16[2,768,384]{2,1,0:T(8,128)(2,1)} %refs_12_.1), channel_id=1, source_target_pairs={{0,1},{1,0},{2,3},{3,2},{4,5},{5,4},{6,7},{7,6},{8,9},{9,8},{10,11... | collective-permute-start | bytes 3538952 | tf_op jit(solution)/shard_map/ppermute | solution.py:1052
  17.4 6.9 %collective-permute-start.2 = (f32[2,6,144,144]{3,2,1,0:T(8,128)}, f32[2,6,144,144]{3,2,1,0:T(8,128)}, u32[]{:S(2)}, u32[]{:S(2)}) collective-permute-start(f32[2,6,144,144]{3,2,1,0:T(8,128)} %refs_6_.4), channel_id=1, source_target_pairs={{0,1},{1,0},{2,3},{3,2},{4,5},{5,4},{6,7},{7,6},{8,9},{9,8},{10,11... | collective-permute-start | bytes 2985992 | tf_op jit(solution)/shard_map/ppermute | solution.py:1052
  60.1 1.5 collective-permute-start.8
  111.3 29.2 %collective-permute-start.10 = (bf16[1792,384]{1,0:T(8,128)(2,1)}, bf16[1792,384]{1,0:T(8,128)(2,1)S(1)}, u32[]{:S(2)}, u32[]{:S(2)}) collective-permute-start(bf16[1792,384]{1,0:T(8,128)(2,1)} %get-tuple-element.116), channel_id=1, source_target_pairs={{0,1},{1,0},{2,3},{3,2},{4,5},{5,4},{6,7},{7,6},{8,9},{9,8},{10,11... | collective-permute-start | bytes 4128776 | tf_op jit(solution)/shard_map/ppermute | solution.py:1052
  138.0 2.6 collective-permute-start.11
  138.2 7.7 %collective-permute-start.12 = (bf16[72,384]{1,0:T(8,128)(2,1)}, bf16[72,384]{1,0:T(8,128)(2,1)S(1)}, u32[]{:S(2)}, u32[]{:S(2)}) collective-permute-start(bf16[72,384]{1,0:T(8,128)(2,1)} %get-tuple-element.119), channel_id=1, source_target_pairs={{0,1},{1,0},{2,3},{3,2},{4,5},{5,4},{6,7},{7,6},{8,9},{9,8},{10,11... | collective-permute-start | bytes 165896 | tf_op jit(solution)/shard_map/ppermute | solution.py:1052
  171.8 3.4 collective-permute-start.13
  179.2 58.6 %collective-permute-start.16 = (bf16[448,384]{1,0:T(8,128)(2,1)}, bf16[448,384]{1,0:T(8,128)(2,1)S(1)}, u32[]{:S(2)}, u32[]{:S(2)}) collective-permute-start(bf16[448,384]{1,0:T(8,128)(2,1)} %get-tuple-element.149), channel_id=1, source_target_pairs={{0,2},{2,0},{4,6},{6,4},{8,10},{10,8},{12,14},{14,12},{16,18},{18,... | collective-permute-start | bytes 1032200 | tf_op jit(solution)/shard_map/ppermute | solution.py:890
  209.0 28.9 %collective-permute-start.17 = (bf16[448,384]{1,0:T(8,128)(2,1)}, bf16[448,384]{1,0:T(8,128)(2,1)S(1)}, u32[]{:S(2)}, u32[]{:S(2)}) collective-permute-start(bf16[448,384]{1,0:T(8,128)(2,1)} %get-tuple-element.150), channel_id=1, source_target_pairs={{0,4},{2,6},{4,0},{6,2},{8,12},{10,14},{12,8},{14,10},{16,20},{18,... | collective-permute-start | bytes 1032200 | tf_op jit(solution)/shard_map/ppermute | solution.py:890
  209.0 28.9 %collective-permute-start.18 = (bf16[448,384]{1,0:T(8,128)(2,1)}, bf16[448,384]{1,0:T(8,128)(2,1)S(1)}, u32[]{:S(2)}, u32[]{:S(2)}) collective-permute-start(bf16[448,384]{1,0:T(8,128)(2,1)} %get-tuple-element.151), channel_id=1, source_target_pairs={{0,6},{2,4},{4,2},{6,0},{8,14},{10,12},{12,10},{14,8},{16,22},{18,... | collective-permute-start | bytes 1032200 | tf_op jit(solution)/shard_map/ppermute | solution.py:890
  237.9 2.6 collective-permute-start.19
  238.0 69.8 %collective-permute-start.15 = (bf16[16,72,384]{2,1,0:T(8,128)(2,1)}, bf16[16,72,384]{2,1,0:T(8,128)(2,1)S(1)}, u32[]{:S(2)}, u32[]{:S(2)}) collective-permute-start(bf16[16,72,384]{2,1,0:T(8,128)(2,1)} %get-tuple-element.144), channel_id=1, source_target_pairs={{0,1},{1,0},{2,3},{3,2},{4,5},{5,4},{6,7},{7,6},{8,9},{9,8},{10,11... | collective-permute-start | bytes 2654216 | tf_op jit(solution)/shard_map/ppermute | solution.py:1052
  238.5 72.7 %collective-permute-start.14 = (bf16[16,72,384]{2,1,0:T(8,128)(2,1)}, bf16[16,72,384]{2,1,0:T(8,128)(2,1)S(1)}, u32[]{:S(2)}, u32[]{:S(2)}) collective-permute-start(bf16[16,72,384]{2,1,0:T(8,128)(2,1)} %get-tuple-element.142), channel_id=1, source_target_pairs={{0,1},{1,0},{2,3},{3,2},{4,5},{5,4},{6,7},{7,6},{8,9},{9,8},{10,11... | collective-permute-start | bytes 2654216 | tf_op jit(solution)/shard_map/ppermute | solution.py:1052
  244.3 11.6 %collective-permute-start.20 = (bf16[112,384]{1,0:T(8,128)(2,1)}, bf16[112,384]{1,0:T(8,128)(2,1)S(1)}, u32[]{:S(2)}, u32[]{:S(2)}) collective-permute-start(bf16[112,384]{1,0:T(8,128)(2,1)} %get-tuple-element.159), channel_id=1, source_target_pairs={{0,8},{2,10},{4,12},{6,14},{8,0},{10,2},{12,4},{14,6},{16,24},{18,... | collective-permute-start | bytes 258056 | tf_op jit(solution)/shard_map/ppermute | solution.py:890
  252.7 8.9 %collective-permute-start.21 = (bf16[112,384]{1,0:T(8,128)(2,1)}, bf16[112,384]{1,0:T(8,128)(2,1)S(1)}, u32[]{:S(2)}, u32[]{:S(2)}) collective-permute-start(bf16[112,384]{1,0:T(8,128)(2,1)} %get-tuple-element.160), channel_id=1, source_target_pairs={{0,16},{2,18},{4,20},{6,22},{8,24},{10,26},{12,28},{14,30},{16,0},... | collective-permute-start | bytes 258056 | tf_op jit(solution)/shard_map/ppermute | solution.py:890
  252.7 8.9 %collective-permute-start.22 = (bf16[112,384]{1,0:T(8,128)(2,1)}, bf16[112,384]{1,0:T(8,128)(2,1)S(1)}, u32[]{:S(2)}, u32[]{:S(2)}) collective-permute-start(bf16[112,384]{1,0:T(8,128)(2,1)} %get-tuple-element.161), channel_id=1, source_target_pairs={{0,24},{2,26},{4,28},{6,30},{8,16},{10,18},{12,20},{14,22},{16,8},... | collective-permute-start | bytes 258056 | tf_op jit(solution)/shard_map/ppermute | solution.py:890
  255.9 16.9 %copy-start.25 = (bf16[112,384]{1,0:T(8,128)(2,1)}, bf16[112,384]{1,0:T(8,128)(2,1)S(1)}, u32[]{:S(2)}) copy-start(bf16[112,384]{1,0:T(8,128)(2,1)S(1)} %collective-permute-done.20.refs_1_) | copy-start | bytes 258052
  255.9 8.6 %collective-permute-start.23 = (bf16[256,384]{1,0:T(8,128)(2,1)}, bf16[256,384]{1,0:T(8,128)(2,1)S(1)}, u32[]{:S(2)}, u32[]{:S(2)}) collective-permute-start(bf16[256,384]{1,0:T(8,128)(2,1)} %get-tuple-element.163), channel_id=1, source_target_pairs={{0,2},{2,0},{4,6},{6,4},{8,10},{10,8},{12,14},{14,12},{16,18},{18,... | collective-permute-start | bytes 589832 | tf_op jit(solution)/shard_map/ppermute | solution.py:890
  261.6 11.2 %copy-start.26 = (bf16[112,384]{1,0:T(8,128)(2,1)}, bf16[112,384]{1,0:T(8,128)(2,1)S(1)}, u32[]{:S(2)}) copy-start(bf16[112,384]{1,0:T(8,128)(2,1)S(1)} %collective-permute-done.21.refs_2_) | copy-start | bytes 258052
  261.6 11.2 %collective-permute-start.24 = (bf16[256,384]{1,0:T(8,128)(2,1)}, bf16[256,384]{1,0:T(8,128)(2,1)S(1)}, u32[]{:S(2)}, u32[]{:S(2)}) collective-permute-start(bf16[256,384]{1,0:T(8,128)(2,1)} %get-tuple-element.164), channel_id=1, source_target_pairs={{0,4},{2,6},{4,0},{6,2},{8,12},{10,14},{12,8},{14,10},{16,20},{18,... | collective-permute-start | bytes 589832 | tf_op jit(solution)/shard_map/ppermute | solution.py:890
  261.6 11.2 %copy-start.27 = (bf16[112,384]{1,0:T(8,128)(2,1)}, bf16[112,384]{1,0:T(8,128)(2,1)S(1)}, u32[]{:S(2)}) copy-start(bf16[112,384]{1,0:T(8,128)(2,1)S(1)} %collective-permute-done.22.refs_3_) | copy-start | bytes 258052
  261.6 11.1 %collective-permute-start.25 = (bf16[256,384]{1,0:T(8,128)(2,1)}, bf16[256,384]{1,0:T(8,128)(2,1)S(1)}, u32[]{:S(2)}, u32[]{:S(2)}) collective-permute-start(bf16[256,384]{1,0:T(8,128)(2,1)} %get-tuple-element.165), channel_id=1, source_target_pairs={{0,6},{2,4},{4,2},{6,0},{8,14},{10,12},{12,10},{14,8},{16,22},{18,... | collective-permute-start | bytes 589832 | tf_op jit(solution)/shard_map/ppermute | solution.py:890
  264.5 8.3 %copy-start.19 = (bf16[256,384]{1,0:T(8,128)(2,1)}, bf16[256,384]{1,0:T(8,128)(2,1)S(1)}, u32[]{:S(2)}) copy-start(bf16[256,384]{1,0:T(8,128)(2,1)S(1)} %collective-permute-done.23.refs_5_) | copy-start | bytes 589828
  275.6 4.4 %collective-permute-start.29 = (bf16[64,384]{1,0:T(8,128)(2,1)}, bf16[64,384]{1,0:T(8,128)(2,1)S(1)}, u32[]{:S(2)}, u32[]{:S(2)}) collective-permute-start(bf16[64,384]{1,0:T(8,128)(2,1)} %get-tuple-element.168), channel_id=1, source_target_pairs={{0,8},{2,10},{4,12},{6,14},{8,0},{10,2},{12,4},{14,6},{16,24},{18,... | collective-permute-start | bytes 147464 | tf_op jit(solution)/shard_map/ppermute | solution.py:890
  275.6 6.2 %collective-permute-start.30 = (bf16[64,384]{1,0:T(8,128)(2,1)}, bf16[64,384]{1,0:T(8,128)(2,1)S(1)}, u32[]{:S(2)}, u32[]{:S(2)}) collective-permute-start(bf16[64,384]{1,0:T(8,128)(2,1)} %get-tuple-element.169), channel_id=1, source_target_pairs={{0,16},{2,18},{4,20},{6,22},{8,24},{10,26},{12,28},{14,30},{16,0},... | collective-permute-start | bytes 147464 | tf_op jit(solution)/shard_map/ppermute | solution.py:890
  276.7 6.9 %collective-permute-start.31 = (bf16[64,384]{1,0:T(8,128)(2,1)}, bf16[64,384]{1,0:T(8,128)(2,1)S(1)}, u32[]{:S(2)}, u32[]{:S(2)}) collective-permute-start(bf16[64,384]{1,0:T(8,128)(2,1)} %get-tuple-element.170), channel_id=1, source_target_pairs={{0,24},{2,26},{4,28},{6,30},{8,16},{10,18},{12,20},{14,22},{16,8},... | collective-permute-start | bytes 147464 | tf_op jit(solution)/shard_map/ppermute | solution.py:890
  280.0 11.2 %copy-start.29 = (bf16[64,384]{1,0:T(8,128)(2,1)}, bf16[64,384]{1,0:T(8,128)(2,1)S(1)}, u32[]{:S(2)}) copy-start(bf16[64,384]{1,0:T(8,128)(2,1)S(1)} %collective-permute-done.29.refs_5_) | copy-start | bytes 147460
  280.0 6.6 %collective-permute-start.26 = (bf16[112,384]{1,0:T(8,128)(2,1)}, bf16[112,384]{1,0:T(8,128)(2,1)S(1)}, u32[]{:S(2)}, u32[]{:S(2)}) collective-permute-start(bf16[112,384]{1,0:T(8,128)(2,1)} %get-tuple-element.166.refs_0_), channel_id=1, source_target_pairs={{0,8},{2,10},{4,12},{6,14},{8,0},{10,2},{12,4},{14,6},{16,24},{18,... | collective-permute-start | bytes 258056 | tf_op jit(solution)/shard_map/ppermute | solution.py:890
  281.8 9.4 %copy-start.30 = (bf16[64,384]{1,0:T(8,128)(2,1)}, bf16[64,384]{1,0:T(8,128)(2,1)S(1)}, u32[]{:S(2)}) copy-start(bf16[64,384]{1,0:T(8,128)(2,1)S(1)} %collective-permute-done.30.refs_6_) | copy-start | bytes 147460
  281.8 9.4 %collective-permute-start.27 = (bf16[112,384]{1,0:T(8,128)(2,1)}, bf16[112,384]{1,0:T(8,128)(2,1)S(1)}, u32[]{:S(2)}, u32[]{:S(2)}) collective-permute-start(bf16[112,384]{1,0:T(8,128)(2,1)} %get-tuple-element.166.refs_0_), channel_id=1, source_target_pairs={{0,16},{2,18},{4,20},{6,22},{8,24},{10,26},{12,28},{14,30},{16,0},... | collective-permute-start | bytes 258056 | tf_op jit(solution)/shard_map/ppermute | solution.py:890
  283.6 7.6 %collective-permute-start.28 = (bf16[112,384]{1,0:T(8,128)(2,1)}, bf16[112,384]{1,0:T(8,128)(2,1)S(1)}, u32[]{:S(2)}, u32[]{:S(2)}) collective-permute-start(bf16[112,384]{1,0:T(8,128)(2,1)} %get-tuple-element.166.refs_0_), channel_id=1, source_target_pairs={{0,24},{2,26},{4,28},{6,30},{8,16},{10,18},{12,20},{14,22},{16,8},... | collective-permute-start | bytes 258056 | tf_op jit(solution)/shard_map/ppermute | solution.py:890
  293.7 5.3 %collective-permute-start.35 = (bf16[64,384]{1,0:T(8,128)(2,1)}, bf16[64,384]{1,0:T(8,128)(2,1)S(1)}, u32[]{:S(2)}, u32[]{:S(2)}) collective-permute-start(bf16[64,384]{1,0:T(8,128)(2,1)} %get-tuple-element.172.refs_0_), channel_id=1, source_target_pairs={{0,8},{2,10},{4,12},{6,14},{8,0},{10,2},{12,4},{14,6},{16,24},{18,... | collective-permute-start | bytes 147464 | tf_op jit(solution)/shard_map/ppermute | solution.py:890
  295.5 5.5 %collective-permute-start.36 = (bf16[64,384]{1,0:T(8,128)(2,1)}, bf16[64,384]{1,0:T(8,128)(2,1)S(1)}, u32[]{:S(2)}, u32[]{:S(2)}) collective-permute-start(bf16[64,384]{1,0:T(8,128)(2,1)} %get-tuple-element.172.refs_0_), channel_id=1, source_target_pairs={{0,16},{2,18},{4,20},{6,22},{8,24},{10,26},{12,28},{14,30},{16,0},... | collective-permute-start | bytes 147464 | tf_op jit(solution)/shard_map/ppermute | solution.py:890
  296.6 6.1 %collective-permute-start.37 = (bf16[64,384]{1,0:T(8,128)(2,1)}, bf16[64,384]{1,0:T(8,128)(2,1)S(1)}, u32[]{:S(2)}, u32[]{:S(2)}) collective-permute-start(bf16[64,384]{1,0:T(8,128)(2,1)} %get-tuple-element.172.refs_0_), channel_id=1, source_target_pairs={{0,24},{2,26},{4,28},{6,30},{8,16},{10,18},{12,20},{14,22},{16,8},... | collective-permute-start | bytes 147464 | tf_op jit(solution)/shard_map/ppermute | solution.py:890
  304.9 8.9 %collective-permute-start.38 = (bf16[256,384]{1,0:T(8,128)(2,1)}, bf16[256,384]{1,0:T(8,128)(2,1)S(1)}, u32[]{:S(2)}, u32[]{:S(2)}) collective-permute-start(bf16[256,384]{1,0:T(8,128)(2,1)} %fold.9.refs_4_), channel_id=1, source_target_pairs={{0,2},{2,0},{4,6},{6,4},{8,10},{10,8},{12,14},{14,12},{16,18},{18,... | collective-permute-start | bytes 589832 | tf_op jit(solution)/shard_map/ppermute | solution.py:890
  307.8 38.2 %collective-permute-start.32 = (bf16[448,384]{1,0:T(8,128)(2,1)}, bf16[448,384]{1,0:T(8,128)(2,1)S(1)}, u32[]{:S(2)}, u32[]{:S(2)}) collective-permute-start(bf16[448,384]{1,0:T(8,128)(2,1)} %get-tuple-element.171.refs_0_), channel_id=1, source_target_pairs={{0,2},{2,0},{4,6},{6,4},{8,10},{10,8},{12,14},{14,12},{16,18},{18,... | collective-permute-start | bytes 1032200 | tf_op jit(solution)/shard_map/ppermute | solution.py:890
  307.8 38.2 %collective-permute-start.33 = (bf16[448,384]{1,0:T(8,128)(2,1)}, bf16[448,384]{1,0:T(8,128)(2,1)S(1)}, u32[]{:S(2)}, u32[]{:S(2)}) collective-permute-start(bf16[448,384]{1,0:T(8,128)(2,1)} %get-tuple-element.171.refs_0_), channel_id=1, source_target_pairs={{0,4},{2,6},{4,0},{6,2},{8,12},{10,14},{12,8},{14,10},{16,20},{18,... | collective-permute-start | bytes 1032200 | tf_op jit(solution)/shard_map/ppermute | solution.py:890
  307.8 38.2 %collective-permute-start.34 = (bf16[448,384]{1,0:T(8,128)(2,1)}, bf16[448,384]{1,0:T(8,128)(2,1)S(1)}, u32[]{:S(2)}, u32[]{:S(2)}) collective-permute-start(bf16[448,384]{1,0:T(8,128)(2,1)} %get-tuple-element.171.refs_0_), channel_id=1, source_target_pairs={{0,6},{2,4},{4,2},{6,0},{8,14},{10,12},{12,10},{14,8},{16,22},{18,... | collective-permute-start | bytes 1032200 | tf_op jit(solution)/shard_map/ppermute | solution.py:890
  311.3 34.7 %collective-permute-start.39 = (bf16[256,384]{1,0:T(8,128)(2,1)}, bf16[256,384]{1,0:T(8,128)(2,1)S(1)}, u32[]{:S(2)}, u32[]{:S(2)}) collective-permute-start(bf16[256,384]{1,0:T(8,128)(2,1)} %fold.9.refs_4_), channel_id=1, source_target_pairs={{0,4},{2,6},{4,0},{6,2},{8,12},{10,14},{12,8},{14,10},{16,20},{18,... | collective-permute-start | bytes 589832 | tf_op jit(solution)/shard_map/ppermute | solution.py:890
  313.8 32.2 %collective-permute-start.40 = (bf16[256,384]{1,0:T(8,128)(2,1)}, bf16[256,384]{1,0:T(8,128)(2,1)S(1)}, u32[]{:S(2)}, u32[]{:S(2)}) collective-permute-start(bf16[256,384]{1,0:T(8,128)(2,1)} %fold.9.refs_4_), channel_id=1, source_target_pairs={{0,6},{2,4},{4,2},{6,0},{8,14},{10,12},{12,10},{14,8},{16,22},{18,... | collective-permute-start | bytes 589832 | tf_op jit(solution)/shard_map/ppermute | solution.py:890
  (31 other events, 76.5 us)
Sparse Core Ops, SparseCore 0:
  172.2 173.7 all-reduce.1
